TPU v7x, 32 devices: a whole 2x2x4 slice. The times are simulated.
32 devices in a mesh: grp: 2 (over x), freq: 16 (over z, y, core).
Axes of the slice: x: 2, y: 2, z: 4, core: 2. Of those that a mesh axis runs over, the one named last changes fastest.
Arguments:
- start_field: bfloat16 [512, 384, 512], P(('grp', 'freq')), parts along dimension 0, may hold values from -2.390625 to 2.390625
- recorded: bfloat16 [32, 384, 4, 128], P(('grp', 'freq')), parts along dimension 0, may hold values from -6 to 6
- multiples: bfloat16 [32, 4, 3, 64, 128], P(('grp', 'freq')), parts along dimension 0, may hold values from -0.3125 to 0.3125
- block_index: int32 [4, 3], replicated, may hold values from 0 to 3, all different within a row
- radius: int32 [512, 384], P(('grp', 'freq')), parts along dimension 0, may hold values from 0 to 4
Outputs:
- field: float32 [512, 384, 512], P(('grp', 'freq')), parts along dimension 0
- residual: float32 [32, 384, 4, 128], P(('grp', 'freq')), parts along dimension 0
There are 2 independent parts, one for each index of `grp`. A program takes and returns all parts, laid end to end along the dimension named above; an argument that names none is the same for every part. Nothing has to cross between parts.
Inputs may be any that keep to these rules, and one draw needn't show every extreme that they name: `block_index`: each row names 3 different source blocks, and every block is named by some row.
All inputs are finite; a program needn't handle non-finite values.
Results may differ from a plain program's by a relative error of at most 0.004.
Values may be sent and summed in bfloat16 or wider, within the bound.
No kernel may reach another device: no remote copies, remote signals or barrier semaphores. Data moves between devices by JAX's collectives and lax.ppermute only.
A program may use at most 64 MiB of HBM per device.

v0:
```python
import math

import jax
import jax.numpy as jnp
from jax import lax
from jax.sharding import PartitionSpec as P

NB = 4
BS = 64
BANDS = 3
NT = 512
RADIUS = 4
ITERS = 2
RECV = 384


step_size = 0.5
shrinkage = 0.05


def extended_2(value, sides, width):
    for axis, dim in sides:
        peers, length = (lax.axis_size(axis), value.shape[dim])
        up = [(i, (i + 1) % peers) for i in range(peers - 1)]
        down = [(j, i) for i, j in up]
        last = lax.slice_in_dim(value, length - width, length, axis=dim)
        leading = lax.slice_in_dim(value, 0, width, axis=dim)
        before = lax.ppermute(last, axis, up)
        after = lax.ppermute(leading, axis, down)
        value = jnp.concatenate([before, value, after], axis=dim)
    return value


def dft_table(freq_count):
    sample_ids = jnp.arange(NT, dtype=jnp.int32)
    bin_ids = jnp.arange(freq_count, dtype=jnp.int32) + 1
    phases = sample_ids[:, None] * bin_ids[None, :] % NT
    angles = phases.astype(jnp.float32) * (2.0 * math.pi / NT)
    stacked = jnp.stack([jnp.cos(angles), -jnp.sin(angles)], axis=-1)
    return stacked.reshape(NT, 2 * freq_count) / math.sqrt(NT)


def embed_complex(multiples):
    real_part = multiples[..., :BS]
    imag_part = multiples[..., BS:]
    upper_rows = jnp.concatenate([real_part, imag_part], axis=-1)
    lower_rows = jnp.concatenate([-imag_part, real_part], axis=-1)
    return jnp.concatenate([upper_rows, lower_rows], axis=-2)


def owner_layout(arrived, freq_count):
    shaped = arrived.reshape(freq_count, 2, NB, BS, arrived.shape[2])
    return shaped.transpose(0, 4, 2, 1, 3).reshape(freq_count, arrived.shape[2], NB, 2 * BS)


def trace_layout(backward, freq_count):
    shaped = backward.reshape(freq_count, backward.shape[1], NB, 2, BS)
    return shaped.transpose(0, 3, 2, 4, 1).reshape(2 * freq_count, NB * BS, backward.shape[1])


def smooth_along(extended, radius, rows_out, along):
    shares = 1.0 / (2.0 * radius.astype(jnp.float32) + 1.0)
    summed = None
    for offset in range(-RADIUS, RADIUS + 1):
        weight = jnp.where(abs(offset) <= radius, shares, 0.0)
        weight = weight[None, :, :]
        piece = lax.slice_in_dim(extended, RADIUS + offset, RADIUS + offset + rows_out, axis=along)
        term = weight * piece.astype(jnp.float32)
        summed = term if summed is None else summed + term
    return summed


def to_time(spectra, basis):
    return jnp.einsum("csr,tc->srt", spectra, basis, precision=lax.Precision.HIGH)


def on_device(start_field, recorded, multiples, block_index, radius):
    devices = lax.axis_size("freq")
    local_freq = recorded.shape[0]
    all_freq = local_freq * devices
    local_src = start_field.shape[0]
    basis = dft_table(all_freq)
    operator = embed_complex(multiples)
    field = start_field.astype(jnp.float32)
    residual = None
    for sweep in range(ITERS):
        spectra = jnp.einsum("srt,tc->csr", field, basis, precision=lax.Precision.HIGH).astype(
            jnp.bfloat16
        )
        arrived = lax.all_to_all(spectra, "freq", split_axis=0, concat_axis=1, tiled=True)
        owned = owner_layout(arrived, local_freq)
        predicted = []
        for out_block in range(NB):
            summed = None
            for band_id in range(BANDS):
                source = lax.dynamic_index_in_dim(
                    owned, block_index[out_block, band_id], axis=2, keepdims=False
                )
                term = jnp.einsum(
                    "frc,fcd->frd",
                    source,
                    operator[:, out_block, band_id],
                    preferred_element_type=jnp.float32,
                )
                summed = term if summed is None else summed + term
            predicted.append(summed)
        residual = recorded.astype(jnp.float32) - jnp.stack(predicted, axis=2)
        narrow = residual.astype(jnp.bfloat16)
        backward = jnp.zeros((local_freq, RECV, NB, 2 * BS), jnp.float32)
        for out_block in range(NB):
            for band_id in range(BANDS):
                contrib = jnp.einsum(
                    "frd,fcd->frc",
                    narrow[:, :, out_block],
                    operator[:, out_block, band_id],
                    preferred_element_type=jnp.float32,
                )
                target_block = block_index[out_block, band_id]
                current = lax.dynamic_index_in_dim(backward, target_block, axis=2, keepdims=False)
                backward = lax.dynamic_update_index_in_dim(
                    backward, current + contrib, target_block, 2
                )
        returned = trace_layout(backward.astype(jnp.bfloat16), local_freq)
        back_spec = lax.all_to_all(returned, "freq", split_axis=1, concat_axis=0, tiled=True)
        with_rim = extended_2(back_spec, (("freq", 1),), RADIUS)
        smoothed_spec = smooth_along(with_rim, radius, local_src, 1)
        smoothed = to_time(smoothed_spec, basis)
        update = field + step_size * smoothed
        field = jnp.sign(update) * jnp.maximum(jnp.abs(update) - shrinkage, 0.0)
    return (field, residual)


def solution(mesh):
    placed = (
        P(("grp", "freq"), None, None),
        P(("grp", "freq"), None, None, None),
        P(("grp", "freq"), None, None, None, None),
        P(),
        P(("grp", "freq"), None),
    )
    return jax.shard_map(
        on_device,
        mesh=mesh,
        in_specs=placed,
        out_specs=(P(("grp", "freq"), None, None), P(("grp", "freq"), None, None, None)),
        check_vma=False,
    )
```

profile of v0, /device:TPU:7, one launch (start us, length us, event | category | flops | bytes accessed | tf_op | source)
XLA Modules:
  0.0 154.5 jit_solution(5975691967619041598)
XLA Ops:
  0.6 0.2 fusion.155
  1.0 6.5 %convolution_convert_fusion.1 = bf16[32,16,384]{2,0,1:T(8,128)(2,1)S(1)} fusion(f32[512,32,1]{0,1,2:T(8,128)S(1)} %reshape.614, bf16[16,384,512]{2,1,0:T(8,128)(2,1)} %param.5), kind=kOutput, calls=%fused_computation.3 | convolution fusion | flops 604176384 | bytes 6750208 | tf_op jit(solution)/shard_map/srt,tc->csr/dot_general | solution.py:87
  7.5 0.9 copy.201
  8.3 6.7 %all-to-all-start = ((bf16[32,16,384]{2,1,0:T(8,128)(2,1)}), bf16[32,16,384]{2,1,0:T(8,128)(2,1)S(1)}, u32[]{:S(2)}, u32[]{:S(2)}) async-start(bf16[32,16,384]{2,1,0:T(8,128)(2,1)} %copy.201), calls=%async_computation | async-start | bytes 786432 | tf_op jit(solution)/shard_map/all_to_all | solution.py:90
  15.0 1.8 %fusion.159 = (s32[1,1]{1,0:T(1,128)}, s32[1,1]{1,0:T(1,128)}, s32[1,1]{1,0:T(1,128)}, s32[1,1]{1,0:T(1,128)}, s32[1,1]{1,0:T(1,128)}, /*index=5*/s32[1,1]{1,0:T...) fusion(s32[4,3]{1,0:T(4,128)} %param.8), kind=kLoop, calls=%fused_computation.291 | loop fusion | bytes 96 | tf_op jit(solution)/shard_map/slice | solution.py:97
  39.9 1.1 slice_negate_fusion
  41.1 1.1 maximum_maximum_fusion
  47.9 0.4 copy.217
  48.4 16.9 %all_to_all.66 = bf16[2,256,384]{2,0,1:T(2,128)(2,1)S(1)} all-to-all(bf16[2,256,384]{2,0,1:T(2,128)(2,1)S(1)} %copy.217), channel_id=1, replica_groups=mesh['grp'=2,'freq'=16] {'freq'}, dimensions={1} | all-to-all | bytes 786432 | tf_op jit(solution)/shard_map/all_to_all | solution.py:124
  65.4 3.2 %collective-permute-start = (bf16[32,4,384]{2,1,0:T(4,128)(2,1)S(1)}, bf16[32,4,384]{2,1,0:T(4,128)(2,1)S(1)}, u32[]{:S(2)}, u32[]{:S(2)}) collective-permute-start(bf16[32,4,384]{2,1,0:T(4,128)(2,1)S(1)} %get-tuple-element.20), channel_id=1, source_target_pairs={{0,1},{1,2},{2,3},{3,4},{4,5},{5,6},{6,7},{7,8},{8,9},{9,10},{10,1... | collective-permute-start | bytes 294920 | tf_op jit(solution)/shard_map/ppermute | solution.py:28
  68.7 2.1 %collective-permute-start.1 = (bf16[32,4,384]{2,1,0:T(4,128)(2,1)S(1)}, bf16[32,4,384]{2,1,0:T(4,128)(2,1)S(1)}, u32[]{:S(2)}, u32[]{:S(2)}) collective-permute-start(bf16[32,4,384]{2,1,0:T(4,128)(2,1)S(1)} %get-tuple-element.21), channel_id=1, source_target_pairs={{1,0},{2,1},{3,2},{4,3},{5,4},{6,5},{7,6},{8,7},{9,8},{10,9},{11,1... | collective-permute-start | bytes 294920 | tf_op jit(solution)/shard_map/ppermute | solution.py:29
  70.8 4.7 %collective-permute-done.1 = bf16[32,4,384]{2,1,0:T(4,128)(2,1)S(1)} collective-permute-done((bf16[32,4,384]{2,1,0:T(4,128)(2,1)S(1)}, bf16[32,4,384]{2,1,0:T(4,128)(2,1)S(1)}, u32[]{:S(2)}, u32[]{:S(2)}) %collective-permute-start.1) | collective-permute-done | bytes 98336 | tf_op jit(solution)/shard_map/ppermute | solution.py:29
  75.5 1.2 multiply_add_fusion.1
  76.8 10.3 %maximum_multiply_fusion.1 = f32[16,384,512]{2,1,0:T(8,128)S(1)} fusion(bf16[16,384,512]{2,1,0:T(8,128)(2,1)S(1)} %bitcast.415, f32[512,32,1]{0,1,2:T(8,128)S(1)} %reshape.614, f32[32,16,384]{2,1,0:T(8,128)S(1)} %multiply_add_fusion.1), kind=kOutput, calls=%fused_computation.1 | convolution fusion | flops 629145600 | bytes 19726336 | tf_op jit(solution)/shard_map/csr,tc->srt/dot_general | solution.py:74
  87.1 6.1 %convolution_convert_fusion = bf16[32,16,384]{2,0,1:T(8,128)(2,1)S(1)} fusion(f32[512,32,1]{0,1,2:T(8,128)S(1)} %reshape.614, f32[16,384,512]{2,1,0:T(8,128)S(1)} %maximum_multiply_fusion.1), kind=kOutput, calls=%fused_computation.2 | convolution fusion | flops 604176384 | bytes 13041664 | tf_op jit(solution)/shard_map/srt,tc->csr/dot_general | solution.py:87
  93.4 14.9 %all_to_all.67 = bf16[32,16,384]{2,1,0:T(8,128)(2,1)S(1)} all-to-all(bf16[32,16,384]{2,1,0:T(8,128)(2,1)S(1)} %copy.221), channel_id=1, replica_groups=mesh['grp'=2,'freq'=16] {'freq'}, dimensions={0} | all-to-all | bytes 786432 | tf_op jit(solution)/shard_map/all_to_all | solution.py:90
  114.1 0.4 copy.237
  114.5 15.5 %all_to_all.68 = bf16[2,256,384]{2,0,1:T(2,128)(2,1)S(1)} all-to-all(bf16[2,256,384]{2,0,1:T(2,128)(2,1)S(1)} %copy.237), channel_id=1, replica_groups=mesh['grp'=2,'freq'=16] {'freq'}, dimensions={1} | all-to-all | bytes 786432 | tf_op jit(solution)/shard_map/all_to_all | solution.py:124
  130.2 3.2 %collective-permute-start.2 = (bf16[32,4,384]{2,1,0:T(4,128)(2,1)S(1)}, bf16[32,4,384]{2,1,0:T(4,128)(2,1)S(1)}, u32[]{:S(2)}, u32[]{:S(2)}) collective-permute-start(bf16[32,4,384]{2,1,0:T(4,128)(2,1)S(1)} %get-tuple-element.18), channel_id=1, source_target_pairs={{0,1},{1,2},{2,3},{3,4},{4,5},{5,6},{6,7},{7,8},{8,9},{9,10},{10,1... | collective-permute-start | bytes 294920 | tf_op jit(solution)/shard_map/ppermute | solution.py:28
  133.5 2.2 %collective-permute-start.3 = (bf16[32,4,384]{2,1,0:T(4,128)(2,1)S(1)}, bf16[32,4,384]{2,1,0:T(4,128)(2,1)S(1)}, u32[]{:S(2)}, u32[]{:S(2)}) collective-permute-start(bf16[32,4,384]{2,1,0:T(4,128)(2,1)S(1)} %get-tuple-element.19), channel_id=1, source_target_pairs={{1,0},{2,1},{3,2},{4,3},{5,4},{6,5},{7,6},{8,7},{9,8},{10,9},{11,1... | collective-permute-start | bytes 294920 | tf_op jit(solution)/shard_map/ppermute | solution.py:29
  135.6 1.4 copy.241
  137.0 3.3 %collective-permute-done.3 = bf16[32,4,384]{2,1,0:T(4,128)(2,1)S(1)} collective-permute-done((bf16[32,4,384]{2,1,0:T(4,128)(2,1)S(1)}, bf16[32,4,384]{2,1,0:T(4,128)(2,1)S(1)}, u32[]{:S(2)}, u32[]{:S(2)}) %collective-permute-start.3) | collective-permute-done | bytes 98336 | tf_op jit(solution)/shard_map/ppermute | solution.py:29
  140.3 1.2 multiply_add_fusion
  141.5 12.9 %maximum_multiply_fusion = f32[16,384,512]{2,1,0:T(8,128)} fusion(f32[16,384,512]{2,1,0:T(8,128)S(1)} %maximum_multiply_fusion.1, f32[512,32,1]{0,1,2:T(8,128)S(1)} %reshape.614, f32[32,16,384]{2,1,0:T(8,128)S(1)} %multiply_add_fusion), kind=kOutput, calls=%fused_computation | convolution fusion | flops 625999872 | bytes 26017792 | tf_op jit(solution)/shard_map/csr,tc->srt/dot_general | solution.py:74
  (106 shorter events, 11.5 us)
Async XLA Ops:
  0.6 44.3 %copy-start = (bf16[1,384,4,128]{3,2,1,0:T(4,128)(2,1)S(1)}, bf16[1,384,4,128]{3,2,1,0:T(4,128)(2,1)}, u32[]{:S(2)}) copy-start(bf16[1,384,4,128]{3,2,1,0:T(4,128)(2,1)} %param.6) | copy-start | bytes 1179652
  8.3 33.8 %all-to-all-start = ((bf16[32,16,384]{2,1,0:T(8,128)(2,1)}), bf16[32,16,384]{2,1,0:T(8,128)(2,1)S(1)}, u32[]{:S(2)}, u32[]{:S(2)}) async-start(bf16[32,16,384]{2,1,0:T(8,128)(2,1)} %copy.201), calls=%async_computation | async-start | bytes 786432 | tf_op jit(solution)/shard_map/all_to_all | solution.py:90
  42.2 28.7 %copy-start.1 = (s32[16,384]{1,0:T(8,128)S(1)}, s32[16,384]{1,0:T(8,128)}, u32[]{:S(2)}) copy-start(s32[16,384]{1,0:T(8,128)} %param.9) | copy-start | bytes 73732
  42.5 34.3 %slice-start = ((s8[6291456]{0:T(1024)(128)(4,1)}), s8[4194304]{0:T(1024)(128)(4,1)S(1)}, s32[]{:S(2)}) async-start(s8[6291456]{0:T(1024)(128)(4,1)} %bitcast.414), calls=%async_computation.4 | async-start | bytes 8388608
  46.5 30.3 %slice-start.1 = ((s8[6291456]{0:T(1024)(128)(4,1)}), s8[2097152]{0:T(1024)(128)(4,1)S(1)}, s32[]{:S(2)}) async-start(s8[6291456]{0:T(1024)(128)(4,1)} %bitcast.414), calls=%async_computation.5 | async-start | bytes 4194304
  65.4 5.4 %collective-permute-start = (bf16[32,4,384]{2,1,0:T(4,128)(2,1)S(1)}, bf16[32,4,384]{2,1,0:T(4,128)(2,1)S(1)}, u32[]{:S(2)}, u32[]{:S(2)}) collective-permute-start(bf16[32,4,384]{2,1,0:T(4,128)(2,1)S(1)} %get-tuple-element.20), channel_id=1, source_target_pairs={{0,1},{1,2},{2,3},{3,4},{4,5},{5,6},{6,7},{7,8},{8,9},{9,10},{10,1... | collective-permute-start | bytes 294920 | tf_op jit(solution)/shard_map/ppermute | solution.py:28
  68.7 6.8 %collective-permute-start.1 = (bf16[32,4,384]{2,1,0:T(4,128)(2,1)S(1)}, bf16[32,4,384]{2,1,0:T(4,128)(2,1)S(1)}, u32[]{:S(2)}, u32[]{:S(2)}) collective-permute-start(bf16[32,4,384]{2,1,0:T(4,128)(2,1)S(1)} %get-tuple-element.21), channel_id=1, source_target_pairs={{1,0},{2,1},{3,2},{4,3},{5,4},{6,5},{7,6},{8,7},{9,8},{10,9},{11,1... | collective-permute-start | bytes 294920 | tf_op jit(solution)/shard_map/ppermute | solution.py:29
  130.2 6.8 %collective-permute-start.2 = (bf16[32,4,384]{2,1,0:T(4,128)(2,1)S(1)}, bf16[32,4,384]{2,1,0:T(4,128)(2,1)S(1)}, u32[]{:S(2)}, u32[]{:S(2)}) collective-permute-start(bf16[32,4,384]{2,1,0:T(4,128)(2,1)S(1)} %get-tuple-element.18), channel_id=1, source_target_pairs={{0,1},{1,2},{2,3},{3,4},{4,5},{5,6},{6,7},{7,8},{8,9},{9,10},{10,1... | collective-permute-start | bytes 294920 | tf_op jit(solution)/shard_map/ppermute | solution.py:28
  133.5 6.8 %collective-permute-start.3 = (bf16[32,4,384]{2,1,0:T(4,128)(2,1)S(1)}, bf16[32,4,384]{2,1,0:T(4,128)(2,1)S(1)}, u32[]{:S(2)}, u32[]{:S(2)}) collective-permute-start(bf16[32,4,384]{2,1,0:T(4,128)(2,1)S(1)} %get-tuple-element.19), channel_id=1, source_target_pairs={{1,0},{2,1},{3,2},{4,3},{5,4},{6,5},{7,6},{8,7},{9,8},{10,9},{11,1... | collective-permute-start | bytes 294920 | tf_op jit(solution)/shard_map/ppermute | solution.py:29
where the time goes:
time: 155 us; the launch traced here: 154 us
  blocking collectives  47.3 us (31%)
  matrix products  45.6 us (29%)
  between operations  24.6 us (16%)
  starting transfers between devices  17.4 us (11%)
  waiting for transfers between devices  7.94 us (5%)
  local copies, waits for them, and re-layouts  6.33 us (4%)
  other arithmetic  5.18 us (3%)
    all_to_all x2, blocking collectives, on_device(): lax.all_to_all(returned, 'freq', split_axis=1, concat_axis=0, tiled=True)  32.4 us
    dot_general x2, matrix products, to_time(): jnp.einsum('csr,tc->srt', spectra, basis, precision=lax.Precision.HIGH)  23.3 us
    all_to_all x1, blocking collectives, on_device(): lax.all_to_all(spectra, 'freq', split_axis=0, concat_axis=1, tiled=True)  14.9 us
    dot_general x2, matrix products, on_device(): jnp.einsum('srt,tc->csr', field, basis, precision=lax.Precision.HIGH)  12.6 us
    ppermute x2, waiting for transfers between devices, extended_2(): after = lax.ppermute(leading, axis, down)  7.93 us
    all_to_all x1, starting transfers between devices, on_device(): lax.all_to_all(spectra, 'freq', split_axis=0, concat_axis=1, tiled=True)  6.67 us
    ppermute x2, starting transfers between devices, extended_2(): before = lax.ppermute(last, axis, up)  6.49 us
    dot_general x24, matrix products, on_device(): jnp.einsum('frc,fcd->frd', source, operator[:, out_block, band_id], prefe...  5.19 us
  transfers between devices with their start and end apart: 5, of which 2 were waited for; matrix products, arithmetic and copies ran while one was open for 4% of the time, Pallas kernels for 0%

commit v1 on v0

v1 whole, which is shorter than its diff:
```python
import math

import jax
import jax.numpy as jnp
import numpy as np
from jax import lax
from jax.experimental import pallas as pl
from jax.experimental.pallas import tpu as pltpu
from jax.sharding import PartitionSpec as P

NB = 4
BS = 64
BANDS = 3
NT = 512
RADIUS = 4
ITERS = 2
STEP = 0.5
SHRINKAGE = 0.05
MIB = 1 << 20


def split_table(freq_count):
    phases = np.arange(NT)[:, None] * (np.arange(freq_count) + 1)[None, :] % NT
    angles = phases * (2.0 * math.pi / NT)
    table = np.stack([np.cos(angles), -np.sin(angles)], axis=-1).reshape(NT, 2 * freq_count) / math.sqrt(NT)
    table = table.T.astype(np.float32)
    upper = table.astype(jnp.bfloat16)
    lower = (table - upper.astype(np.float32)).astype(jnp.bfloat16)
    return np.concatenate([upper, lower], axis=0)


def contract(a, b, dims):
    return lax.dot_general(a, b, ((dims[:1], dims[1:]), ((), ())), preferred_element_type=jnp.float32)


def shrink(u):
    return u - jnp.clip(u, -SHRINKAGE, SHRINKAGE)


def params(semantics, limit):
    return pltpu.CompilerParams(dimension_semantics=(semantics,), vmem_limit_bytes=limit * MIB)


def rows_per_step(rows, receivers):
    step = receivers
    while step * 2 <= 1024 and rows % (step * 2) == 0:
        step *= 2
    return step


def forward_kernel(field_ref, table_ref, spectra_ref):
    half = spectra_ref.shape[0]
    both = contract(table_ref[...], field_ref[...], (1, 1))
    spectra_ref[...] = (both[:half] + both[half:]).astype(jnp.bfloat16)


def forward(field, table, receivers):
    rows = field.shape[0]
    step = rows_per_step(rows, receivers)
    count = table.shape[0] // 2
    return pl.pallas_call(
        forward_kernel,
        grid=(rows // step,),
        in_specs=[pl.BlockSpec((step, NT), lambda i: (i, 0)), pl.BlockSpec(table.shape, lambda i: (0, 0))],
        out_specs=pl.BlockSpec((count, step), lambda i: (0, i)),
        out_shape=jax.ShapeDtypeStruct((count, rows), jnp.bfloat16),
        compiler_params=params("arbitrary", 16),
        cost_estimate=pl.CostEstimate(flops=4 * rows * NT * count, bytes_accessed=2 * rows * NT, transcendentals=0),
        name="forward_dft",
    )(field, table)


def gradient_of(spectra_ref, half_table_ref):
    spectra = spectra_ref[...]
    return contract(jnp.concatenate([spectra, spectra], axis=0), half_table_ref[...], (0, 0))


def middle_kernel(start_ref, spectra_ref, table_ref, half_table_ref, field_ref, out_ref):
    count = out_ref.shape[0]
    field = shrink(start_ref[...].astype(jnp.float32) + gradient_of(spectra_ref, half_table_ref))
    field_ref[...] = field
    upper = field.astype(jnp.bfloat16)
    lower = (field - upper.astype(jnp.float32)).astype(jnp.bfloat16)
    both = contract(table_ref[...], upper, (1, 1))
    rest = contract(table_ref[:count], lower, (1, 1))
    out_ref[...] = (both[:count] + (both[count:] + rest)).astype(jnp.bfloat16)


def middle(start, spectra, table, half_table, receivers):
    rows = start.shape[0]
    step = rows_per_step(rows, receivers)
    count = table.shape[0] // 2
    return pl.pallas_call(
        middle_kernel,
        grid=(rows // step,),
        in_specs=[
            pl.BlockSpec((step, NT), lambda i: (i, 0)),
            pl.BlockSpec((count, step), lambda i: (0, i)),
            pl.BlockSpec(table.shape, lambda i: (0, 0)),
            pl.BlockSpec(half_table.shape, lambda i: (0, 0)),
        ],
        out_specs=[pl.BlockSpec((step, NT), lambda i: (i, 0)), pl.BlockSpec((count, step), lambda i: (0, i))],
        out_shape=[jax.ShapeDtypeStruct((rows, NT), jnp.float32), jax.ShapeDtypeStruct((count, rows), jnp.bfloat16)],
        compiler_params=params("arbitrary", 24),
        cost_estimate=pl.CostEstimate(flops=10 * rows * NT * count, bytes_accessed=6 * rows * NT, transcendentals=0),
        name="update_and_forward",
    )(start, spectra, table, half_table)


def final_kernel(field_ref, spectra_ref, half_table_ref, out_ref):
    out_ref[...] = shrink(field_ref[...] + gradient_of(spectra_ref, half_table_ref))


def final(field, spectra, half_table, receivers):
    rows = field.shape[0]
    step = rows_per_step(rows, receivers)
    count = half_table.shape[0] // 2
    return pl.pallas_call(
        final_kernel,
        grid=(rows // step,),
        in_specs=[
            pl.BlockSpec((step, NT), lambda i: (i, 0)),
            pl.BlockSpec((count, step), lambda i: (0, i)),
            pl.BlockSpec(half_table.shape, lambda i: (0, 0)),
        ],
        out_specs=pl.BlockSpec((step, NT), lambda i: (i, 0)),
        out_shape=jax.ShapeDtypeStruct((rows, NT), jnp.float32),
        compiler_params=params("arbitrary", 24),
        cost_estimate=pl.CostEstimate(flops=4 * rows * NT * count, bytes_accessed=8 * rows * NT, transcendentals=0),
        name="last_update",
    )(field, spectra, half_table)


def owner_kernel(index_ref, arrived_ref, recorded_ref, multiples_ref, radius_ref, *rest):
    returned_ref, operator, padded = rest[0], rest[-2], rest[-1]
    sources = NB * BS
    operator[...] = jnp.zeros_like(operator)
    for block in range(NB):
        columns = slice(block * 2 * BS, (block + 1) * 2 * BS)
        for band in range(BANDS):
            first = pl.multiple_of(index_ref[block, band] * BS, BS)
            pair = multiples_ref[0, block, band]
            operator[pl.ds(first, BS), columns] = pair
            operator[pl.ds(sources + first, BS), columns] = jnp.concatenate([-pair[:, BS:], pair[:, :BS]], axis=1)
    table = operator[...]
    residual = recorded_ref[0].astype(jnp.float32) - contract(arrived_ref[0], table, (0, 0))
    if len(rest) == 4:
        rest[1][0] = residual
    backward = contract(table, residual.astype(jnp.bfloat16), (1, 1))
    radius = radius_ref[...]
    shares = 1.0 / (2.0 * radius.astype(jnp.float32) + 1.0)
    for part in range(2):
        own = backward[part * sources : (part + 1) * sources]
        padded[: 2 * RADIUS] = jnp.zeros_like(padded[: 2 * RADIUS])
        padded[2 * RADIUS + sources :] = jnp.zeros_like(padded[: 2 * RADIUS])
        padded[2 * RADIUS : 2 * RADIUS + sources] = own
        summed = own
        for offset in range(1, RADIUS + 1):
            low = padded[2 * RADIUS - offset : 2 * RADIUS - offset + sources]
            high = padded[2 * RADIUS + offset : 2 * RADIUS + offset + sources]
            summed = summed + jnp.where(radius >= offset, low + high, 0.0)
        returned_ref[0, part] = (summed * shares).astype(jnp.bfloat16)


def owner(arrived, recorded, multiples, block_index, radius, with_residual):
    count, _, receivers = arrived.shape
    sources = NB * BS
    wide = NB * 2 * BS
    out_specs = [pl.BlockSpec((1, 2, sources, receivers), lambda i: (i, 0, 0, 0))]
    out_shape = [jax.ShapeDtypeStruct((count, 2, sources, receivers), jnp.bfloat16)]
    if with_residual:
        out_specs.append(pl.BlockSpec((1, receivers, wide), lambda i: (i, 0, 0)))
        out_shape.append(jax.ShapeDtypeStruct((count, receivers, wide), jnp.float32))
    return pl.pallas_call(
        owner_kernel,
        grid=(count,),
        in_specs=[
            pl.BlockSpec(memory_space=pltpu.SMEM),
            pl.BlockSpec((1, 2 * sources, receivers), lambda i: (i, 0, 0)),
            pl.BlockSpec((1, receivers, wide), lambda i: (i, 0, 0)),
            pl.BlockSpec((1, NB, BANDS, BS, 2 * BS), lambda i: (i, 0, 0, 0, 0)),
            pl.BlockSpec((sources, receivers), lambda i: (0, 0)),
        ],
        out_specs=out_specs,
        out_shape=out_shape,
        scratch_shapes=[
            pltpu.VMEM((2 * sources, wide), jnp.bfloat16),
            pltpu.VMEM((sources + 4 * RADIUS, receivers), jnp.float32),
        ],
        compiler_params=params("arbitrary", 24),
        cost_estimate=pl.CostEstimate(
            flops=8 * count * receivers * sources * wide, bytes_accessed=6 * count * receivers * wide, transcendentals=0
        ),
        name="owner_step",
    )(block_index, arrived, recorded, multiples, radius)


def on_device(start_field, recorded, multiples, block_index, radius):
    devices = lax.axis_size("freq")
    local_freq = recorded.shape[0]
    all_freq = local_freq * devices
    local_src, receivers, _ = start_field.shape
    rows = local_src * receivers
    table = jnp.asarray(split_table(all_freq))
    half_table = table * STEP
    start = start_field.reshape(rows, NT)
    recorded = recorded.reshape(local_freq, receivers, NB * 2 * BS)
    radius = lax.all_gather(radius, "freq", axis=0, tiled=True)
    field, residual = start, None
    spectra = forward(start, table, receivers)
    for sweep in range(ITERS):
        last = sweep == ITERS - 1
        arrived = lax.all_to_all(
            spectra.reshape(2 * all_freq, local_src, receivers), "freq", split_axis=0, concat_axis=1, tiled=True
        )
        outs = owner(
            arrived.reshape(local_freq, 2 * NB * BS, receivers), recorded, multiples, block_index, radius, last
        )
        returned = lax.all_to_all(
            outs[0].reshape(2 * local_freq, NB * BS, receivers), "freq", split_axis=1, concat_axis=0, tiled=True
        ).reshape(2 * all_freq, rows)
        if last:
            field = final(field, returned, half_table, receivers)
            residual = outs[1]
        else:
            field, spectra = middle(field, returned, table, half_table, receivers)
    return (
        field.reshape(local_src, receivers, NT),
        residual.reshape(local_freq, receivers, NB, 2 * BS),
    )


def solution(mesh):
    placed = (
        P(("grp", "freq"), None, None),
        P(("grp", "freq"), None, None, None),
        P(("grp", "freq"), None, None, None, None),
        P(),
        P(("grp", "freq"), None),
    )
    return jax.shard_map(
        on_device,
        mesh=mesh,
        in_specs=placed,
        out_specs=(P(("grp", "freq"), None, None), P(("grp", "freq"), None, None, None)),
        check_vma=False,
    )
```

time: 155 us -> 121 us (0.78)
  the two profiles are of different devices: /device:TPU:7 before, /device:TPU:0 now
where the time goes in v1:
time: 121 us
  blocking collectives  53.7 us (44%)
  local copies, waits for them, and re-layouts  22.4 us (19%)
  Pallas kernels  21.8 us (18%)
  waiting for transfers between devices  11 us (9%)
  starting transfers between devices  10.9 us (9%)
    all_gather x1, blocking collectives, on_device(): radius = lax.all_gather(radius, 'freq', axis=0, tiled=True)  23.1 us
    unnamed x26, local copies, waits for them, and re-layouts  18.4 us
    all_to_all x1, blocking collectives, on_device(): lax.all_to_all(spectra.reshape(2 * all_freq, local_src, receivers), 'freq...  15.5 us
    all_to_all x1, blocking collectives, on_device(): lax.all_to_all(outs[0].reshape(2 * local_freq, NB * BS, receivers), 'freq...  15.1 us
    all_to_all x1, waiting for transfers between devices, on_device(): lax.all_to_all(outs[0].reshape(2 * local_freq, NB * BS, receivers), 'freq...  11 us
    pallas_call x1, Pallas kernels, middle(): pl.pallas_call(middle_kernel, grid=(rows // step,), in_specs=[pl.BlockSpe...  7.56 us
    all_to_all x1, starting transfers between devices, on_device(): lax.all_to_all(spectra.reshape(2 * all_freq, local_src, receivers), 'freq...  7.39 us
    pallas_call x1, Pallas kernels, final(): pl.pallas_call(final_kernel, grid=(rows // step,), in_specs=[pl.BlockSpec...  6.67 us
  transfers between devices with their start and end apart: 2, of which 1 were waited for; matrix products, arithmetic and copies ran while one was open for 2% of the time, Pallas kernels for 0%

profile of v1, /device:TPU:0, one launch (start us, length us, event | category | flops | bytes accessed | tf_op | source)
XLA Modules:
  0.0 120.7 jit_solution(17886707045934085911)
XLA Ops:
  0.6 2.8 %copy-done = bf16[16,384,512]{2,1,0:T(8,128)(2,1)S(1)} copy-done((bf16[16,384,512]{2,1,0:T(8,128)(2,1)S(1)}, bf16[16,384,512]{2,1,0:T(8,128)(2,1)}, u32[]{:S(2)}) %copy-start) | copy-done | bytes 6291480
  3.4 0.8 copy-done.5
  4.3 3.0 %forward_dft.1 = bf16[32,6144]{1,0:T(8,128)(2,1)S(1)} custom-call(bf16[6144,512]{1,0:T(8,128)(2,1)S(1)} %bitcast.26, bf16[64,512]{1,0:T(8,128)(2,1)S(1)} %copy-done.5), custom_call_target="tpu_custom_call" | custom-call | flops 402653184 | bytes 6291456 | tf_op jit(solution)/shard_map/forward_dft/pallas_call | solution.py:61
  7.3 0.8 copy.20
  8.1 7.4 %all-to-all-start = ((bf16[32,16,384]{2,1,0:T(8,128)(2,1)}), bf16[32,16,384]{2,1,0:T(8,128)(2,1)S(1)}, u32[]{:S(2)}, u32[]{:S(2)}) async-start(bf16[32,16,384]{2,1,0:T(8,128)(2,1)} %bitcast.17), calls=%async_computation | async-start | bytes 786432 | tf_op jit(solution)/shard_map/all_to_all | solution.py:213
  15.5 1.1 reshape.47.recorded_ref
  16.6 23.1 %all_gather.3.radius_ref = s32[256,384]{1,0:T(8,128)S(1)} all-gather(s32[16,384]{1,0:T(8,128)} %param.10), channel_id=1, replica_groups=mesh['grp'=2,'freq'=16] {'freq'}, dimensions={0}, use_global_device_ids=true | all-gather | bytes 417792 | tf_op jit(solution)/shard_map/all_gather | solution.py:208
  39.7 0.9 copy-done.7
  40.7 0.7 copy-done.9
  41.3 2.3 %owner_step.2 = bf16[1,2,256,384]{3,2,1,0:T(8,128)(2,1)S(1)} custom-call(s32[4,3]{1,0:T(4,128)S(1)} %copy-done.9, bf16[1,512,384]{2,1,0:T(8,128)(2,1)S(1)} %bitcast.29, bf16[1,384,512]{2,1,0:T(8,128)(2,1)S(1)} %reshape.47.recorded_ref, bf16[1,4,3,64,128]{4,3,2,1,0:T(8,128)(2,1)S(1)} %copy-done.7, s32[256,384]{1,0:T(8,128)S(1)} %all_gather.3.radius_ref), custom_call_target="tpu_custom_call" | custom-call | flops 402653184 | bytes 1179648 | tf_op jit(solution)/shard_map/owner_step/pallas_call | solution.py:174
  43.6 0.4 copy.15
  44.1 15.1 %all_to_all.60 = bf16[2,256,384]{2,0,1:T(2,128)(2,1)S(1)} all-to-all(bf16[2,256,384]{2,0,1:T(2,128)(2,1)S(1)} %copy.15), channel_id=1, replica_groups=mesh['grp'=2,'freq'=16] {'freq'}, dimensions={1} | all-to-all | bytes 786432 | tf_op jit(solution)/shard_map/all_to_all | solution.py:219
  59.3 2.8 %copy-done.1 = bf16[16,384,512]{2,1,0:T(8,128)(2,1)S(1)} copy-done((bf16[16,384,512]{2,1,0:T(8,128)(2,1)S(1)}, bf16[16,384,512]{2,1,0:T(8,128)(2,1)}, u32[]{:S(2)}) %copy-start.1) | copy-done | bytes 6291480
  62.1 7.6 %update_and_forward.1 = (f32[6144,512]{1,0:T(8,128)S(1)}, bf16[32,6144]{1,0:T(8,128)(2,1)S(1)}) custom-call(bf16[6144,512]{1,0:T(8,128)(2,1)S(1)} %bitcast.27, bf16[32,6144]{1,0:T(8,128)(2,1)S(1)} %bitcast.31, bf16[64,512]{1,0:T(8,128)(2,1)S(1)} %copy-done.6, bf16[64,512]{1,0:T(8,128)(2,1)S(1)} %copy-done.4), custom_call_target="tpu_custom_call" | custom-call | flops 1006632960 | bytes 18874368 | tf_op jit(solution)/shard_map/update_and_forward/pallas_call | solution.py:93
  69.7 4.8 %copy-done.2 = f32[6144,512]{1,0:T(8,128)} copy-done((f32[6144,512]{1,0:T(8,128)}, f32[6144,512]{1,0:T(8,128)S(1)}, u32[]{:S(2)}) %copy-start.2) | copy-done | bytes 12582936
  74.5 15.5 %all_to_all.61 = bf16[32,16,384]{2,1,0:T(8,128)(2,1)S(1)} all-to-all(bf16[32,16,384]{2,1,0:T(8,128)(2,1)S(1)} %bitcast.41), channel_id=1, replica_groups=mesh['grp'=2,'freq'=16] {'freq'}, dimensions={0} | all-to-all | bytes 786432 | tf_op jit(solution)/shard_map/all_to_all | solution.py:213
  90.1 2.3 %owner_step.3 = (bf16[1,2,256,384]{3,2,1,0:T(8,128)(2,1)S(1)}, f32[1,384,512]{2,1,0:T(8,128)S(1)}) custom-call(s32[4,3]{1,0:T(4,128)S(1)} %copy-done.10, bf16[1,512,384]{2,1,0:T(8,128)(2,1)S(1)} %bitcast.33, bf16[1,384,512]{2,1,0:T(8,128)(2,1)S(1)} %reshape.47.recorded_ref, bf16[1,4,3,64,128]{4,3,2,1,0:T(8,128)(2,1)S(1)} %copy-done.8, ...), custom_call_target="tpu_custom_call" | custom-call | flops 402653184 | bytes 1179648 | tf_op jit(solution)/shard_map/owner_step/pallas_call | solution.py:174
  92.4 1.2 copy.18
  93.6 3.6 %all-to-all-start.3 = ((bf16[2,256,384]{2,0,1:T(2,128)(2,1)}), bf16[2,256,384]{2,0,1:T(2,128)(2,1)S(1)}, u32[]{:S(2)}, u32[]{:S(2)}) async-start(bf16[2,256,384]{2,0,1:T(2,128)(2,1)} %copy.18), calls=%async_computation.3 | async-start | bytes 786432 | tf_op jit(solution)/shard_map/all_to_all | solution.py:219
  97.1 1.1 reshape.55
  98.3 11.0 %all-to-all-done.3 = bf16[2,256,384]{2,0,1:T(2,128)(2,1)S(1)} async-done(((bf16[2,256,384]{2,0,1:T(2,128)(2,1)}), bf16[2,256,384]{2,0,1:T(2,128)(2,1)S(1)}, u32[]{:S(2)}, u32[]{:S(2)}) %all-to-all-start.3) | async-done | bytes 393248 | tf_op jit(solution)/shard_map/all_to_all | solution.py:219
  109.3 0.1 copy.23
  109.4 4.6 %copy-done.3 = f32[6144,512]{1,0:T(8,128)S(1)} copy-done((f32[6144,512]{1,0:T(8,128)S(1)}, f32[6144,512]{1,0:T(8,128)}, u32[]{:S(2)}) %copy-start.3) | copy-done | bytes 12582936
  114.0 6.7 %last_update.1 = f32[6144,512]{1,0:T(8,128)} custom-call(f32[6144,512]{1,0:T(8,128)S(1)} %copy-done.3, bf16[32,6144]{1,0:T(8,128)(2,1)S(1)} %bitcast.32, bf16[64,512]{1,0:T(8,128)(2,1)S(1)} %copy-done.4), custom_call_target="tpu_custom_call" | custom-call | flops 402653184 | bytes 25165824 | tf_op jit(solution)/shard_map/last_update/pallas_call | solution.py:118
  (22 shorter events, 0.4 us)
Async XLA Ops:
  0.6 2.8 %copy-start = (bf16[16,384,512]{2,1,0:T(8,128)(2,1)S(1)}, bf16[16,384,512]{2,1,0:T(8,128)(2,1)}, u32[]{:S(2)}) copy-start(bf16[16,384,512]{2,1,0:T(8,128)(2,1)} %param.6) | copy-start | bytes 18874372
  3.4 0.8 copy-start.5
  4.3 55.0 %copy-start.4 = (bf16[64,512]{1,0:T(8,128)(2,1)S(1)}, bf16[64,512]{1,0:T(8,128)(2,1)}, u32[]{:S(2)}) copy-start(bf16[64,512]{1,0:T(8,128)(2,1)} %constant.9.half_table_ref) | copy-start | bytes 196612
  4.3 55.0 %copy-start.6 = (bf16[64,512]{1,0:T(8,128)(2,1)S(1)}, bf16[64,512]{1,0:T(8,128)(2,1)}, u32[]{:S(2)}) copy-start(bf16[64,512]{1,0:T(8,128)(2,1)} %constant.4.clone.table_ref) | copy-start | bytes 196612
  4.3 85.8 %copy-start.8 = (bf16[1,4,3,64,128]{4,3,2,1,0:T(8,128)(2,1)S(1)}, bf16[1,4,3,64,128]{4,3,2,1,0:T(8,128)(2,1)}, u32[]{:S(2)}) copy-start(bf16[1,4,3,64,128]{4,3,2,1,0:T(8,128)(2,1)} %multiples_ref.3) | copy-start | bytes 589828
  4.3 85.8 %copy-start.10 = (s32[4,3]{1,0:T(4,128)S(1)}, s32[4,3]{1,0:T(4,128)}, u32[]{:S(2)}) copy-start(s32[4,3]{1,0:T(4,128)} %index_ref.3) | copy-start | bytes 148
  8.1 31.6 %all-to-all-start = ((bf16[32,16,384]{2,1,0:T(8,128)(2,1)}), bf16[32,16,384]{2,1,0:T(8,128)(2,1)S(1)}, u32[]{:S(2)}, u32[]{:S(2)}) async-start(bf16[32,16,384]{2,1,0:T(8,128)(2,1)} %bitcast.17), calls=%async_computation | async-start | bytes 786432 | tf_op jit(solution)/shard_map/all_to_all | solution.py:213
  39.7 0.9 copy-start.7
  40.7 0.7 copy-start.9
  59.3 2.8 %copy-start.1 = (bf16[16,384,512]{2,1,0:T(8,128)(2,1)S(1)}, bf16[16,384,512]{2,1,0:T(8,128)(2,1)}, u32[]{:S(2)}) copy-start(bf16[16,384,512]{2,1,0:T(8,128)(2,1)} %param.6) | copy-start | bytes 18874372
  69.7 4.8 %copy-start.2 = (f32[6144,512]{1,0:T(8,128)}, f32[6144,512]{1,0:T(8,128)S(1)}, u32[]{:S(2)}) copy-start(f32[6144,512]{1,0:T(8,128)S(1)} %get-tuple-element.6.field_ref) | copy-start | bytes 37748740
  93.6 15.7 %all-to-all-start.3 = ((bf16[2,256,384]{2,0,1:T(2,128)(2,1)}), bf16[2,256,384]{2,0,1:T(2,128)(2,1)S(1)}, u32[]{:S(2)}, u32[]{:S(2)}) async-start(bf16[2,256,384]{2,0,1:T(2,128)(2,1)} %copy.18), calls=%async_computation.3 | async-start | bytes 786432 | tf_op jit(solution)/shard_map/all_to_all | solution.py:219
  109.4 4.6 %copy-start.3 = (f32[6144,512]{1,0:T(8,128)S(1)}, f32[6144,512]{1,0:T(8,128)}, u32[]{:S(2)}) copy-start(f32[6144,512]{1,0:T(8,128)} %copy-done.2) | copy-start | bytes 37748740

commit v2 on v0

v2 whole, which is shorter than its diff:
```python
import math

import jax
import jax.numpy as jnp
import numpy as np
from jax import lax
from jax.experimental import pallas as pl
from jax.experimental.pallas import tpu as pltpu
from jax.sharding import PartitionSpec as P

NB = 4
BS = 64
BANDS = 3
NT = 512
RADIUS = 4
STEP = 0.5
SHRINKAGE = 0.05
SOURCES = NB * BS
WIDE = NB * 2 * BS
MIB = 1 << 20
VMEM = pl.BlockSpec(memory_space=pltpu.VMEM)
ANY = pl.BlockSpec(memory_space=pl.ANY)


def split_table(freq_count):
    phases = np.arange(NT)[:, None] * (np.arange(freq_count) + 1)[None, :] % NT
    angles = phases * (2.0 * math.pi / NT)
    table = np.stack([np.cos(angles), -np.sin(angles)], axis=-1).reshape(NT, 2 * freq_count) / math.sqrt(NT)
    table = table.T.astype(np.float32)
    upper = table.astype(jnp.bfloat16)
    lower = (table - upper.astype(np.float32)).astype(jnp.bfloat16)
    return np.concatenate([upper, lower], axis=0)


def contract(a, b, dims):
    return lax.dot_general(a, b, ((dims[:1], dims[1:]), ((), ())), preferred_element_type=jnp.float32)


def clamp(u):
    return jnp.clip(u, -SHRINKAGE, SHRINKAGE)


def params(limit):
    return pltpu.CompilerParams(vmem_limit_bytes=limit * MIB)


def chunk_rows(rows, most):
    return max(size for size in range(128, most + 1, 128) if rows % size == 0)


def build_operator(index_ref, multiples_ref, operator_ref):
    operator_ref[...] = jnp.zeros_like(operator_ref)
    for block in range(NB):
        columns = slice(block * 2 * BS, (block + 1) * 2 * BS)
        for band in range(BANDS):
            first = pl.multiple_of(index_ref[block, band] * BS, BS)
            pair = multiples_ref[block, band]
            operator_ref[pl.ds(first, BS), columns] = pair
            operator_ref[pl.ds(SOURCES + first, BS), columns] = jnp.concatenate([-pair[:, BS:], pair[:, :BS]], axis=1)


def forward_kernel(
    field_hbm, table_hbm, index_hbm, multiples_hbm, recorded_hbm, radius_hbm,
    narrow_ref, spectra_ref, field_ref, table_ref, operator_ref, recorded_ref, radius_ref,
    index, multiples, loaded, unpacked, radius, sems, field_sems,
):
    receivers = recorded_ref.shape[0]
    count, rows = spectra_ref.shape
    step = rows // field_sems.shape[0]
    small = [
        pltpu.make_async_copy(index_hbm, index, sems.at[0]),
        pltpu.make_async_copy(multiples_hbm, multiples, sems.at[1]),
        pltpu.make_async_copy(recorded_hbm, loaded, sems.at[2]),
        pltpu.make_async_copy(table_hbm, table_ref, sems.at[3]),
        pltpu.make_async_copy(radius_hbm, radius, sems.at[4]),
    ]
    for copy in small:
        copy.start()
    large = []
    for i in range(rows // step):
        part = pl.ds(i * step, step)
        large.append(pltpu.make_async_copy(field_hbm.at[part], field_ref.at[part], field_sems.at[i]))
        large[-1].start()
    small[0].wait()
    small[1].wait()
    build_operator(index, multiples, operator_ref)
    small[2].wait()
    unpacked[...] = loaded[...].astype(jnp.float32)
    for block in range(NB):
        recorded_ref[:, block * 2 * BS : (block + 1) * 2 * BS] = unpacked[pl.ds(block, receivers, stride=NB), :]
    small[4].wait()
    radius_ref[...] = radius[...].astype(jnp.float32).astype(jnp.bfloat16)
    small[3].wait()
    for i in range(rows // step):
        part = slice(i * step, (i + 1) * step)
        large[i].wait()
        both = contract(table_ref[...], field_ref[part], (1, 1))
        spectra = both[:count] + both[count:]
        spectra_ref[:, part] = spectra
        narrow_ref[:, part] = spectra.astype(jnp.bfloat16)


def forward(field, table, block_index, multiples, recorded, radius):
    rows, receivers = field.shape[0], radius.shape[1]
    step = chunk_rows(rows, 1024)
    count = table.shape[0] // 2
    arguments = (field, table, block_index, multiples, recorded, radius)
    return pl.pallas_call(
        forward_kernel,
        in_specs=[ANY] * 6,
        out_specs=[VMEM] * 7,
        out_shape=[
            jax.ShapeDtypeStruct((count, rows), jnp.bfloat16),
            pltpu.VMEM((count, rows), jnp.float32),
            pltpu.VMEM((rows, NT), jnp.bfloat16),
            pltpu.VMEM(table.shape, jnp.bfloat16),
            pltpu.VMEM((2 * SOURCES, WIDE), jnp.bfloat16),
            pltpu.VMEM((receivers, WIDE), jnp.float32),
            jax.ShapeDtypeStruct(radius.shape, jnp.bfloat16),
        ],
        scratch_shapes=[
            pltpu.SMEM((NB, BANDS), jnp.int32),
            pltpu.VMEM((NB, BANDS, BS, 2 * BS), jnp.bfloat16),
            pltpu.VMEM((receivers * NB, 2 * BS), jnp.bfloat16),
            pltpu.VMEM((receivers * NB, 2 * BS), jnp.float32),
            pltpu.VMEM(radius.shape, jnp.int32),
            pltpu.SemaphoreType.DMA((5,)),
            pltpu.SemaphoreType.DMA((rows // step,)),
        ],
        compiler_params=params(16),
        name="forward_dft",
    )(*(pltpu.with_memory_space_constraint(a, pltpu.HBM) for a in arguments))


def gradient_of(returned_ref, table_ref, part):
    returned = returned_ref[:, part]
    return contract(jnp.concatenate([returned, returned], axis=0), table_ref[...], (0, 0))


def middle_kernel(start_ref, returned_ref, spectra_ref, table_ref, field_ref, narrow_ref, *, step):
    count, rows = spectra_ref.shape
    for i in range(rows // step):
        part = slice(i * step, (i + 1) * step)
        update = start_ref[part].astype(jnp.float32) + gradient_of(returned_ref, table_ref, part)
        clamped = clamp(update)
        field_ref[part] = update - clamped
        both = contract(table_ref[...], clamped.astype(jnp.bfloat16), (1, 1))
        linear = spectra_ref[:, part] + 0.5 * returned_ref[:, part].astype(jnp.float32)
        narrow_ref[:, part] = (linear - (both[:count] + both[count:])).astype(jnp.bfloat16)


def middle(start, returned, spectra, table):
    rows = start.shape[0]
    step = chunk_rows(rows, 768)
    return pl.pallas_call(
        lambda *refs: middle_kernel(*refs, step=step),
        in_specs=[VMEM] * 4,
        out_specs=[VMEM] * 2,
        out_shape=[pltpu.VMEM((rows, NT), jnp.float32), jax.ShapeDtypeStruct(spectra.shape, jnp.bfloat16)],
        compiler_params=params(16),
        name="update_and_forward",
    )(start, returned, spectra, table)


def final_kernel(field_ref, returned_ref, table_ref, out_hbm, buffer, sems):
    slots, step, _ = buffer.shape
    rows = field_ref.shape[0]
    copies = []
    for i in range(rows // step):
        if i >= slots:
            copies[i - slots].wait()
        part = slice(i * step, (i + 1) * step)
        update = field_ref[part] + gradient_of(returned_ref, table_ref, part)
        buffer[i % slots] = update - clamp(update)
        copies.append(
            pltpu.make_async_copy(buffer.at[i % slots], out_hbm.at[pl.ds(i * step, step)], sems.at[i % slots])
        )
        copies[i].start()
    for copy in copies[-slots:]:
        copy.wait()


def final(field, returned, table):
    rows = field.shape[0]
    step = chunk_rows(rows, 512)
    slots = min(4, rows // step)
    return pl.pallas_call(
        final_kernel,
        in_specs=[VMEM] * 3,
        out_specs=ANY,
        out_shape=pltpu.HBM((rows, NT), jnp.float32),
        scratch_shapes=[pltpu.VMEM((slots, step, NT), jnp.float32), pltpu.SemaphoreType.DMA((slots,))],
        compiler_params=params(16),
        name="last_update",
    )(field, returned, table)


def owner_kernel(arrived_ref, operator_ref, recorded_ref, radius_ref, returned_ref, *rest):
    with_residual = len(rest) > 1
    padded = rest[1] if with_residual else rest[0]
    receivers = recorded_ref.shape[0]
    operator = operator_ref[...]
    residual = recorded_ref[...] - contract(arrived_ref[...], operator, (0, 0))
    if with_residual:
        residual_hbm, _, interleaved, sem = rest
        for block in range(NB):
            interleaved[pl.ds(block, receivers, stride=NB), :] = residual[:, block * 2 * BS : (block + 1) * 2 * BS]
        copy = pltpu.make_async_copy(interleaved, residual_hbm, sem)
        copy.start()
    backward = contract(operator, residual.astype(jnp.bfloat16), (1, 1))
    radius = radius_ref[...].astype(jnp.float32)
    shares = STEP / (2.0 * radius + 1.0)
    edge = jnp.zeros((2 * RADIUS, receivers), jnp.float32)
    for part in range(2):
        own = backward[part * SOURCES : (part + 1) * SOURCES]
        padded[part, : 2 * RADIUS] = edge
        padded[part, 2 * RADIUS + SOURCES :] = edge
        padded[part, 2 * RADIUS : 2 * RADIUS + SOURCES] = own
        summed = own
        for offset in range(1, RADIUS + 1):
            low = padded[part, 2 * RADIUS - offset : 2 * RADIUS - offset + SOURCES]
            high = padded[part, 2 * RADIUS + offset : 2 * RADIUS + offset + SOURCES]
            summed = summed + jnp.where(radius >= offset, low + high, 0.0)
        returned_ref[part * SOURCES : (part + 1) * SOURCES] = (summed * shares).astype(jnp.bfloat16)
    if with_residual:
        copy.wait()


def owner(arrived, operator, recorded, radius, with_residual):
    receivers = arrived.shape[1]
    out_shape = [jax.ShapeDtypeStruct((2 * SOURCES, receivers), jnp.bfloat16)]
    scratch = [pltpu.VMEM((2, SOURCES + 4 * RADIUS, receivers), jnp.float32)]
    if with_residual:
        out_shape.append(pltpu.HBM((receivers * NB, 2 * BS), jnp.float32))
        scratch += [pltpu.VMEM((receivers * NB, 2 * BS), jnp.float32), pltpu.SemaphoreType.DMA(())]
    return pl.pallas_call(
        owner_kernel,
        in_specs=[VMEM] * 4,
        out_specs=[VMEM, ANY][: len(out_shape)],
        out_shape=out_shape,
        scratch_shapes=scratch,
        compiler_params=params(16),
        name="owner_step",
    )(arrived, operator, recorded, radius)


def exchange(pieces):
    return lax.all_to_all(pieces, "freq", split_axis=0, concat_axis=0, tiled=True)


def on_device(start_field, recorded, multiples, block_index, radius):
    devices = lax.axis_size("freq")
    local_src, receivers, _ = start_field.shape
    rows = local_src * receivers
    table = jnp.asarray(split_table(devices))

    def to_owners(narrow, extra=None):
        pieces = narrow.reshape(devices, 2, local_src, receivers)
        if extra is not None:
            extra = jnp.broadcast_to(extra, (devices, 1, local_src, receivers))
            pieces = jnp.concatenate([pieces, extra], axis=1)
        arrived = exchange(pieces).swapaxes(0, 1)
        return arrived.reshape(arrived.shape[0] * SOURCES, receivers)

    def to_traces(returned):
        pieces = returned.reshape(2, devices, local_src, receivers).swapaxes(0, 1)
        return exchange(pieces).reshape(2 * devices, rows)

    narrow, spectra, start, table, operator, recorded, radius = forward(
        start_field.reshape(rows, NT), table, block_index, multiples[0], recorded.reshape(-1, 2 * BS), radius
    )
    arrived = to_owners(narrow, radius)
    radius = arrived[2 * SOURCES :]
    (returned,) = owner(arrived[: 2 * SOURCES], operator, recorded, radius, False)
    field, narrow = middle(start, to_traces(returned), spectra, table)
    returned, residual = owner(to_owners(narrow), operator, recorded, radius, True)
    field = final(field, to_traces(returned), table)
    return field.reshape(local_src, receivers, NT), residual.reshape(1, receivers, NB, 2 * BS)


def solution(mesh):
    placed = (
        P(("grp", "freq"), None, None),
        P(("grp", "freq"), None, None, None),
        P(("grp", "freq"), None, None, None, None),
        P(),
        P(("grp", "freq"), None),
    )
    return jax.shard_map(
        on_device,
        mesh=mesh,
        in_specs=placed,
        out_specs=(P(("grp", "freq"), None, None), P(("grp", "freq"), None, None, None)),
        check_vma=False,
    )
```

time: 155 us -> 89 us (0.57)
  the two profiles are of different devices: /device:TPU:7 before, /device:TPU:0 now
where the time goes in v2:
time: 89 us; the launch traced here: 88.7 us
  blocking collectives  70.5 us (79%)
  Pallas kernels  16.9 us (19%)
    all_to_all x4, blocking collectives, exchange(): lax.all_to_all(pieces, 'freq', split_axis=0, concat_axis=0, tiled=True)  70.5 us
    pallas_call x1, Pallas kernels, forward(): pl.pallas_call(forward_kernel, in_specs=[ANY] * 6, out_specs=[VMEM] * 7,...  5.27 us
    pallas_call x1, Pallas kernels, final(): pl.pallas_call(final_kernel, in_specs=[VMEM] * 3, out_specs=ANY, out_shap...  4.99 us
    pallas_call x1, Pallas kernels, middle(): pl.pallas_call(lambda *refs: middle_kernel(*refs, step=step), in_specs=[V...  3.41 us
    pallas_call x2, Pallas kernels, owner(): pl.pallas_call(owner_kernel, in_specs=[VMEM] * 4, out_specs=[VMEM, ANY][:...  3.27 us

profile of v2, /device:TPU:0, one launch (start us, length us, event | category | flops | bytes accessed | tf_op | source)
XLA Modules:
  0.0 88.7 jit_solution(11120942837687961472)
XLA Ops:
  0.6 5.3 %forward_dft.1 = (bf16[32,6144]{1,0:T(8,128)(2,1)S(1)}, f32[32,6144]{1,0:T(8,128)S(1)}, bf16[6144,512]{1,0:T(8,128)(2,1)S(1)}, bf16[64,512]{1,0:T(8,128)(2,1)S(1...) custom-call(bf16[6144,512]{1,0:T(8,128)(2,1)} %bitcast.41, ...), custom_call_target="tpu_custom_call" | custom-call | tf_op jit(solution)/shard_map/forward_dft/pallas_call | solution.py:108
  6.0 0.1 pad_maximum_fusion
  6.1 24.5 %all_to_all.20 = bf16[16,3,16,384]{3,2,1,0:T(8,128)(2,1)S(1)} all-to-all(bf16[16,3,16,384]{3,2,1,0:T(8,128)(2,1)S(1)} %pad_maximum_fusion), channel_id=1, replica_groups=mesh['grp'=2,'freq'=16] {'freq'}, dimensions={0} | all-to-all | bytes 1179648 | tf_op jit(solution)/shard_map/all_to_all | solution.py:248
  30.7 1.6 %owner_step.2 = bf16[512,384]{1,0:T(8,128)(2,1)S(1)} custom-call(bf16[512,384]{1,0:T(8,128)(2,1)S(1)} %bitcast.33, bf16[512,512]{1,0:T(8,128)(2,1)S(1)} %get-tuple-element.16.operator_ref, f32[384,512]{1,0:T(8,128)S(1)} %get-tuple-element.17.recorded_ref, bf16[256,384]{1,0:T(8,128)(2,1)S(1)} %bitcast.30), custom_call_target="tpu_custom_call" | custom-call | tf_op jit(solution)/shard_map/owner_step/pallas_call | solution.py:236
  32.4 15.0 %all_to_all.21 = bf16[16,2,16,384]{3,2,1,0:T(8,128)(2,1)S(1)} all-to-all(bf16[16,2,16,384]{3,2,1,0:T(8,128)(2,1)S(1)} %bitcast.44), channel_id=1, replica_groups=mesh['grp'=2,'freq'=16] {'freq'}, dimensions={0} | all-to-all | bytes 786432 | tf_op jit(solution)/shard_map/all_to_all | solution.py:248
  47.3 0.1 copy.17
  47.4 3.4 %update_and_forward.1 = (f32[6144,512]{1,0:T(8,128)S(1)}, bf16[32,6144]{1,0:T(8,128)(2,1)S(1)}) custom-call(bf16[6144,512]{1,0:T(8,128)(2,1)S(1)} %get-tuple-element.13.refs_0_, bf16[32,6144]{1,0:T(8,128)(2,1)S(1)} %bitcast.32, f32[32,6144]{1,0:T(8,128)S(1)} %get-tuple-element.18.refs_2_, bf16[64,512]{1,0:T(8,128)(2,1)S(1)} %get-tuple-element.19.refs_3_.table_ref), custom_call_target="tpu_custom_call" | custom-call | tf_op jit(solution)/shard_map/update_and_forward/pallas_call | solution.py:155
  50.9 15.5 %all_to_all.22 = bf16[16,2,16,384]{3,2,1,0:T(8,128)(2,1)S(1)} all-to-all(bf16[16,2,16,384]{3,2,1,0:T(8,128)(2,1)S(1)} %bitcast.46), channel_id=1, replica_groups=mesh['grp'=2,'freq'=16] {'freq'}, dimensions={0} | all-to-all | bytes 786432 | tf_op jit(solution)/shard_map/all_to_all | solution.py:248
  66.5 1.6 %owner_step.3 = (bf16[512,384]{1,0:T(8,128)(2,1)S(1)}, f32[1536,128]{1,0:T(8,128)}) custom-call(bf16[512,384]{1,0:T(8,128)(2,1)S(1)} %bitcast.35, bf16[512,512]{1,0:T(8,128)(2,1)S(1)} %get-tuple-element.16.operator_ref, f32[384,512]{1,0:T(8,128)S(1)} %get-tuple-element.17.recorded_ref, bf16[256,384]{1,0:T(8,128)(2,1)S(1)} %bitcast.31), custom_call_target="tpu_custom_call" | custom-call | tf_op jit(solution)/shard_map/owner_step/pallas_call | solution.py:236
  68.2 15.5 %all_to_all.23 = bf16[16,2,16,384]{3,2,1,0:T(8,128)(2,1)S(1)} all-to-all(bf16[16,2,16,384]{3,2,1,0:T(8,128)(2,1)S(1)} %bitcast.48), channel_id=1, replica_groups=mesh['grp'=2,'freq'=16] {'freq'}, dimensions={0} | all-to-all | bytes 786432 | tf_op jit(solution)/shard_map/all_to_all | solution.py:248
  83.7 0.1 copy.19
  83.8 5.0 %last_update.1 = f32[6144,512]{1,0:T(8,128)} custom-call(f32[6144,512]{1,0:T(8,128)S(1)} %get-tuple-element.20.field_ref, bf16[32,6144]{1,0:T(8,128)(2,1)S(1)} %bitcast.36, bf16[64,512]{1,0:T(8,128)(2,1)S(1)} %get-tuple-element.19.refs_3_.table_ref), custom_call_target="tpu_custom_call" | custom-call | tf_op jit(solution)/shard_map/last_update/pallas_call | solution.py:187
  (9 shorter events, 0.3 us)

commit v3 on v2

--- a/solution.py
+++ b/solution.py
@@ -48,6 +48,12 @@
     return max(size for size in range(128, most + 1, 128) if rows % size == 0)
 
 
+def chunks(rows):
+    unit = rows // 128 // 6 * 128
+    bounds = [0, unit, 2 * unit, 4 * unit, rows] if unit else [0, rows]
+    return [slice(low, high) for low, high in zip(bounds[:-1], bounds[1:])]
+
+
 def build_operator(index_ref, multiples_ref, operator_ref):
     operator_ref[...] = jnp.zeros_like(operator_ref)
     for block in range(NB):
@@ -66,43 +72,47 @@
 ):
     receivers = recorded_ref.shape[0]
     count, rows = spectra_ref.shape
-    step = rows // field_sems.shape[0]
+    parts = chunks(rows)
     small = [
-        pltpu.make_async_copy(index_hbm, index, sems.at[0]),
-        pltpu.make_async_copy(multiples_hbm, multiples, sems.at[1]),
-        pltpu.make_async_copy(recorded_hbm, loaded, sems.at[2]),
-        pltpu.make_async_copy(table_hbm, table_ref, sems.at[3]),
+        pltpu.make_async_copy(table_hbm, table_ref, sems.at[0]),
+        pltpu.make_async_copy(index_hbm, index, sems.at[1]),
+        pltpu.make_async_copy(multiples_hbm, multiples, sems.at[2]),
+        pltpu.make_async_copy(recorded_hbm, loaded, sems.at[3]),
         pltpu.make_async_copy(radius_hbm, radius, sems.at[4]),
     ]
-    for copy in small:
+    large = []
+    for i, part in enumerate(parts):
+        place = pl.ds(part.start, part.stop - part.start)
+        large.append(pltpu.make_async_copy(field_hbm.at[place], field_ref.at[place], field_sems.at[i]))
+    for copy in small[:1] + large[:2] + small[1:] + large[2:]:
         copy.start()
-    large = []
-    for i in range(rows // step):
-        part = pl.ds(i * step, step)
-        large.append(pltpu.make_async_copy(field_hbm.at[part], field_ref.at[part], field_sems.at[i]))
-        large[-1].start()
+
+    def transform(i):
+        large[i].wait()
+        both = contract(table_ref[...], field_ref[parts[i]], (1, 1))
+        spectra = both[:count] + both[count:]
+        spectra_ref[:, parts[i]] = spectra
+        narrow_ref[:, parts[i]] = spectra.astype(jnp.bfloat16)
+
     small[0].wait()
+    transform(0)
     small[1].wait()
+    small[2].wait()
     build_operator(index, multiples, operator_ref)
-    small[2].wait()
+    for i in range(1, len(parts) // 2):
+        transform(i)
+    small[3].wait()
     unpacked[...] = loaded[...].astype(jnp.float32)
     for block in range(NB):
         recorded_ref[:, block * 2 * BS : (block + 1) * 2 * BS] = unpacked[pl.ds(block, receivers, stride=NB), :]
     small[4].wait()
     radius_ref[...] = radius[...].astype(jnp.float32).astype(jnp.bfloat16)
-    small[3].wait()
-    for i in range(rows // step):
-        part = slice(i * step, (i + 1) * step)
-        large[i].wait()
-        both = contract(table_ref[...], field_ref[part], (1, 1))
-        spectra = both[:count] + both[count:]
-        spectra_ref[:, part] = spectra
-        narrow_ref[:, part] = spectra.astype(jnp.bfloat16)
+    for i in range(max(1, len(parts) // 2), len(parts)):
+        transform(i)
 
 
 def forward(field, table, block_index, multiples, recorded, radius):
     rows, receivers = field.shape[0], radius.shape[1]
-    step = chunk_rows(rows, 1024)
     count = table.shape[0] // 2
     arguments = (field, table, block_index, multiples, recorded, radius)
     return pl.pallas_call(
@@ -125,7 +135,7 @@
             pltpu.VMEM((receivers * NB, 2 * BS), jnp.float32),
             pltpu.VMEM(radius.shape, jnp.int32),
             pltpu.SemaphoreType.DMA((5,)),
-            pltpu.SemaphoreType.DMA((rows // step,)),
+            pltpu.SemaphoreType.DMA((len(chunks(rows)),)),
         ],
         compiler_params=params(16),
         name="forward_dft",
@@ -195,33 +205,35 @@
     )(field, returned, table)
 
 
+def smooth(backward, radius):
+    sources, receivers = radius.shape
+    rows = jnp.concatenate([backward[:sources], backward[sources:]], axis=1)
+    narrow = rows.astype(jnp.bfloat16)
+    radius = jnp.concatenate([radius, radius], axis=1)
+    distance = jnp.abs(
+        lax.broadcasted_iota(jnp.int32, (sources, sources), 0) - lax.broadcasted_iota(jnp.int32, (sources, sources), 1)
+    )
+    summed = rows
+    for width in range(1, RADIUS + 1):
+        band = jnp.where(distance <= width, 1.0, 0.0).astype(jnp.bfloat16)
+        summed = jnp.where(radius >= width, contract(band, narrow, (1, 0)), summed)
+    smoothed = (summed * (STEP / (2.0 * radius + 1.0))).astype(jnp.bfloat16)
+    return jnp.concatenate([smoothed[:, :receivers], smoothed[:, receivers:]], axis=0)
+
+
 def owner_kernel(arrived_ref, operator_ref, recorded_ref, radius_ref, returned_ref, *rest):
-    with_residual = len(rest) > 1
-    padded = rest[1] if with_residual else rest[0]
+    with_residual = len(rest) > 0
     receivers = recorded_ref.shape[0]
     operator = operator_ref[...]
     residual = recorded_ref[...] - contract(arrived_ref[...], operator, (0, 0))
     if with_residual:
-        residual_hbm, _, interleaved, sem = rest
+        residual_hbm, interleaved, sem = rest
         for block in range(NB):
             interleaved[pl.ds(block, receivers, stride=NB), :] = residual[:, block * 2 * BS : (block + 1) * 2 * BS]
         copy = pltpu.make_async_copy(interleaved, residual_hbm, sem)
         copy.start()
     backward = contract(operator, residual.astype(jnp.bfloat16), (1, 1))
-    radius = radius_ref[...].astype(jnp.float32)
-    shares = STEP / (2.0 * radius + 1.0)
-    edge = jnp.zeros((2 * RADIUS, receivers), jnp.float32)
-    for part in range(2):
-        own = backward[part * SOURCES : (part + 1) * SOURCES]
-        padded[part, : 2 * RADIUS] = edge
-        padded[part, 2 * RADIUS + SOURCES :] = edge
-        padded[part, 2 * RADIUS : 2 * RADIUS + SOURCES] = own
-        summed = own
-        for offset in range(1, RADIUS + 1):
-            low = padded[part, 2 * RADIUS - offset : 2 * RADIUS - offset + SOURCES]
-            high = padded[part, 2 * RADIUS + offset : 2 * RADIUS + offset + SOURCES]
-            summed = summed + jnp.where(radius >= offset, low + high, 0.0)
-        returned_ref[part * SOURCES : (part + 1) * SOURCES] = (summed * shares).astype(jnp.bfloat16)
+    returned_ref[...] = smooth(backward, radius_ref[...].astype(jnp.float32))
     if with_residual:
         copy.wait()
 
@@ -229,10 +241,10 @@
 def owner(arrived, operator, recorded, radius, with_residual):
     receivers = arrived.shape[1]
     out_shape = [jax.ShapeDtypeStruct((2 * SOURCES, receivers), jnp.bfloat16)]
-    scratch = [pltpu.VMEM((2, SOURCES + 4 * RADIUS, receivers), jnp.float32)]
+    scratch = []
     if with_residual:
         out_shape.append(pltpu.HBM((receivers * NB, 2 * BS), jnp.float32))
-        scratch += [pltpu.VMEM((receivers * NB, 2 * BS), jnp.float32), pltpu.SemaphoreType.DMA(())]
+        scratch = [pltpu.VMEM((receivers * NB, 2 * BS), jnp.float32), pltpu.SemaphoreType.DMA(())]
     return pl.pallas_call(
         owner_kernel,
         in_specs=[VMEM] * 4,

time: 89 us -> 87.2 us (0.980)
  Pallas kernels: 16.9 us -> 15.1 us
    pallas_call x1, Pallas kernels: 5.27 us -> 4.11 us  [forward(): pl.pallas_call(forward_kernel, in_specs=[ANY] * 6, out_specs=[VMEM] * 7,...]
where the time goes in v3:
time: 87.2 us; the launch traced here: 86.9 us
  blocking collectives  70.5 us (81%)
  Pallas kernels  15.1 us (17%)
    all_to_all x4, blocking collectives, exchange(): lax.all_to_all(pieces, 'freq', split_axis=0, concat_axis=0, tiled=True)  70.5 us
    pallas_call x1, Pallas kernels, final(): pl.pallas_call(final_kernel, in_specs=[VMEM] * 3, out_specs=ANY, out_shap...  4.99 us
    pallas_call x1, Pallas kernels, forward(): pl.pallas_call(forward_kernel, in_specs=[ANY] * 6, out_specs=[VMEM] * 7,...  4.11 us
    pallas_call x1, Pallas kernels, middle(): pl.pallas_call(lambda *refs: middle_kernel(*refs, step=step), in_specs=[V...  3.41 us
    pallas_call x2, Pallas kernels, owner(): pl.pallas_call(owner_kernel, in_specs=[VMEM] * 4, out_specs=[VMEM, ANY][:...  2.61 us

profile of v3, /device:TPU:0, one launch (start us, length us, event | category | flops | bytes accessed | tf_op | source)
XLA Modules:
  0.0 86.9 jit_solution(12878273405316970966)
XLA Ops:
  0.6 4.1 %forward_dft.1 = (bf16[32,6144]{1,0:T(8,128)(2,1)S(1)}, f32[32,6144]{1,0:T(8,128)S(1)}, bf16[6144,512]{1,0:T(8,128)(2,1)S(1)}, bf16[64,512]{1,0:T(8,128)(2,1)S(1...) custom-call(bf16[6144,512]{1,0:T(8,128)(2,1)} %bitcast.41, ...), custom_call_target="tpu_custom_call" | custom-call | tf_op jit(solution)/shard_map/forward_dft/pallas_call | solution.py:118
  4.8 0.1 pad_maximum_fusion
  4.9 24.5 %all_to_all.20 = bf16[16,3,16,384]{3,2,1,0:T(8,128)(2,1)S(1)} all-to-all(bf16[16,3,16,384]{3,2,1,0:T(8,128)(2,1)S(1)} %pad_maximum_fusion), channel_id=1, replica_groups=mesh['grp'=2,'freq'=16] {'freq'}, dimensions={0} | all-to-all | bytes 1179648 | tf_op jit(solution)/shard_map/all_to_all | solution.py:260
  29.5 1.3 %owner_step.2 = bf16[512,384]{1,0:T(8,128)(2,1)S(1)} custom-call(bf16[512,384]{1,0:T(8,128)(2,1)S(1)} %bitcast.33, bf16[512,512]{1,0:T(8,128)(2,1)S(1)} %get-tuple-element.16.operator_ref, f32[384,512]{1,0:T(8,128)S(1)} %get-tuple-element.17.recorded_ref, bf16[256,384]{1,0:T(8,128)(2,1)S(1)} %bitcast.30), custom_call_target="tpu_custom_call" | custom-call | tf_op jit(solution)/shard_map/owner_step/pallas_call | solution.py:248
  30.9 15.0 %all_to_all.21 = bf16[16,2,16,384]{3,2,1,0:T(8,128)(2,1)S(1)} all-to-all(bf16[16,2,16,384]{3,2,1,0:T(8,128)(2,1)S(1)} %bitcast.44), channel_id=1, replica_groups=mesh['grp'=2,'freq'=16] {'freq'}, dimensions={0} | all-to-all | bytes 786432 | tf_op jit(solution)/shard_map/all_to_all | solution.py:260
  45.9 0.1 copy.17
  45.9 3.4 %update_and_forward.1 = (f32[6144,512]{1,0:T(8,128)S(1)}, bf16[32,6144]{1,0:T(8,128)(2,1)S(1)}) custom-call(bf16[6144,512]{1,0:T(8,128)(2,1)S(1)} %get-tuple-element.13.refs_0_, bf16[32,6144]{1,0:T(8,128)(2,1)S(1)} %bitcast.32, f32[32,6144]{1,0:T(8,128)S(1)} %get-tuple-element.18.refs_2_, bf16[64,512]{1,0:T(8,128)(2,1)S(1)} %get-tuple-element.19.refs_3_.table_ref), custom_call_target="tpu_custom_call" | custom-call | tf_op jit(solution)/shard_map/update_and_forward/pallas_call | solution.py:165
  49.4 15.5 %all_to_all.22 = bf16[16,2,16,384]{3,2,1,0:T(8,128)(2,1)S(1)} all-to-all(bf16[16,2,16,384]{3,2,1,0:T(8,128)(2,1)S(1)} %bitcast.46), channel_id=1, replica_groups=mesh['grp'=2,'freq'=16] {'freq'}, dimensions={0} | all-to-all | bytes 786432 | tf_op jit(solution)/shard_map/all_to_all | solution.py:260
  65.0 1.3 %owner_step.3 = (bf16[512,384]{1,0:T(8,128)(2,1)S(1)}, f32[1536,128]{1,0:T(8,128)}) custom-call(bf16[512,384]{1,0:T(8,128)(2,1)S(1)} %bitcast.35, bf16[512,512]{1,0:T(8,128)(2,1)S(1)} %get-tuple-element.16.operator_ref, f32[384,512]{1,0:T(8,128)S(1)} %get-tuple-element.17.recorded_ref, bf16[256,384]{1,0:T(8,128)(2,1)S(1)} %bitcast.31), custom_call_target="tpu_custom_call" | custom-call | tf_op jit(solution)/shard_map/owner_step/pallas_call | solution.py:248
  66.3 15.5 %all_to_all.23 = bf16[16,2,16,384]{3,2,1,0:T(8,128)(2,1)S(1)} all-to-all(bf16[16,2,16,384]{3,2,1,0:T(8,128)(2,1)S(1)} %bitcast.48), channel_id=1, replica_groups=mesh['grp'=2,'freq'=16] {'freq'}, dimensions={0} | all-to-all | bytes 786432 | tf_op jit(solution)/shard_map/all_to_all | solution.py:260
  81.8 0.1 copy.19
  81.9 5.0 %last_update.1 = f32[6144,512]{1,0:T(8,128)} custom-call(f32[6144,512]{1,0:T(8,128)S(1)} %get-tuple-element.20.field_ref, bf16[32,6144]{1,0:T(8,128)(2,1)S(1)} %bitcast.36, bf16[64,512]{1,0:T(8,128)(2,1)S(1)} %get-tuple-element.19.refs_3_.table_ref), custom_call_target="tpu_custom_call" | custom-call | tf_op jit(solution)/shard_map/last_update/pallas_call | solution.py:197
  (9 shorter events, 0.3 us)

commit v4 on v3

--- a/solution.py
+++ b/solution.py
@@ -14,6 +14,7 @@
 NT = 512
 RADIUS = 4
 STEP = 0.5
+MARK = 8
 SHRINKAGE = 0.05
 SOURCES = NB * BS
 WIDE = NB * 2 * BS
@@ -221,36 +222,70 @@
     return jnp.concatenate([smoothed[:, :receivers], smoothed[:, receivers:]], axis=0)
 
 
-def owner_kernel(arrived_ref, operator_ref, recorded_ref, radius_ref, returned_ref, *rest):
-    with_residual = len(rest) > 0
-    receivers = recorded_ref.shape[0]
+def adjoint(arrived_ref, operator_ref, recorded_ref):
     operator = operator_ref[...]
     residual = recorded_ref[...] - contract(arrived_ref[...], operator, (0, 0))
-    if with_residual:
-        residual_hbm, interleaved, sem = rest
-        for block in range(NB):
-            interleaved[pl.ds(block, receivers, stride=NB), :] = residual[:, block * 2 * BS : (block + 1) * 2 * BS]
-        copy = pltpu.make_async_copy(interleaved, residual_hbm, sem)
-        copy.start()
-    backward = contract(operator, residual.astype(jnp.bfloat16), (1, 1))
+    return residual, contract(operator, residual.astype(jnp.bfloat16), (1, 1))
+
+
+def first_owner_kernel(arrived_ref, operator_ref, recorded_ref, backward_ref):
+    _, backward_ref[...] = adjoint(arrived_ref, operator_ref, recorded_ref)
+
+
+def smooth_kernel(backward_ref, radius_ref, returned_ref):
+    returned_ref[...] = smooth(backward_ref[...], radius_ref[...].astype(jnp.float32))
+
+
+def last_owner_kernel(
+    arrived_ref, operator_ref, recorded_ref, radius_ref, returned_ref, residual_hbm, interleaved, sem
+):
+    residual, backward = adjoint(arrived_ref, operator_ref, recorded_ref)
+    for block in range(NB):
+        rows = pl.ds(block, residual.shape[0], stride=NB)
+        interleaved[rows, :] = residual[:, block * 2 * BS : (block + 1) * 2 * BS]
+    copy = pltpu.make_async_copy(interleaved, residual_hbm, sem)
+    copy.start()
     returned_ref[...] = smooth(backward, radius_ref[...].astype(jnp.float32))
-    if with_residual:
-        copy.wait()
-
-
-def owner(arrived, operator, recorded, radius, with_residual):
+    copy.wait()
+
+
+def first_owner(arrived, operator, recorded):
     receivers = arrived.shape[1]
-    out_shape = [jax.ShapeDtypeStruct((2 * SOURCES, receivers), jnp.bfloat16)]
-    scratch = []
-    if with_residual:
-        out_shape.append(pltpu.HBM((receivers * NB, 2 * BS), jnp.float32))
-        scratch = [pltpu.VMEM((receivers * NB, 2 * BS), jnp.float32), pltpu.SemaphoreType.DMA(())]
-    return pl.pallas_call(
-        owner_kernel,
+    return pl.pallas_call(
+        first_owner_kernel,
+        in_specs=[VMEM] * 3,
+        out_specs=VMEM,
+        out_shape=pltpu.VMEM((2 * SOURCES, receivers), jnp.float32),
+        compiler_params=params(16),
+        cost_estimate=pl.CostEstimate(
+            flops=8 * receivers * SOURCES * WIDE, bytes_accessed=8 * receivers * WIDE, transcendentals=0
+        ),
+        name="owner_products",
+    )(arrived, operator, recorded)
+
+
+def smooth_sources(backward, radius):
+    return pl.pallas_call(
+        smooth_kernel,
+        in_specs=[VMEM] * 2,
+        out_specs=VMEM,
+        out_shape=jax.ShapeDtypeStruct(backward.shape, jnp.bfloat16),
+        compiler_params=params(16),
+        name="smooth_sources",
+    )(backward, radius)
+
+
+def last_owner(arrived, operator, recorded, radius):
+    receivers = arrived.shape[1]
+    return pl.pallas_call(
+        last_owner_kernel,
         in_specs=[VMEM] * 4,
-        out_specs=[VMEM, ANY][: len(out_shape)],
-        out_shape=out_shape,
-        scratch_shapes=scratch,
+        out_specs=[VMEM, ANY],
+        out_shape=[
+            jax.ShapeDtypeStruct((2 * SOURCES, receivers), jnp.bfloat16),
+            pltpu.HBM((receivers * NB, 2 * BS), jnp.float32),
+        ],
+        scratch_shapes=[pltpu.VMEM((receivers * NB, 2 * BS), jnp.float32), pltpu.SemaphoreType.DMA(())],
         compiler_params=params(16),
         name="owner_step",
     )(arrived, operator, recorded, radius)
@@ -266,13 +301,28 @@
     rows = local_src * receivers
     table = jnp.asarray(split_table(devices))
 
-    def to_owners(narrow, extra=None):
-        pieces = narrow.reshape(devices, 2, local_src, receivers)
-        if extra is not None:
-            extra = jnp.broadcast_to(extra, (devices, 1, local_src, receivers))
-            pieces = jnp.concatenate([pieces, extra], axis=1)
-        arrived = exchange(pieces).swapaxes(0, 1)
-        return arrived.reshape(arrived.shape[0] * SOURCES, receivers)
+    def by_part(arrived):
+        return arrived.reshape(devices, 2, local_src, receivers).swapaxes(0, 1).reshape(2 * SOURCES, receivers)
+
+    def to_owners(narrow):
+        return by_part(exchange(narrow.reshape(devices, 2, local_src, receivers)))
+
+    def to_owners_with_radius(narrow, radius):
+        shares = 2 if devices % 2 == 0 and local_src % 2 == 0 else 1
+        rows = local_src // shares
+        marked = radius.reshape(shares, rows, receivers) + MARK * jnp.arange(shares, dtype=radius.dtype)[:, None, None]
+        marked = jnp.broadcast_to(marked, (devices // shares, shares, rows, receivers))
+        narrow = lax.optimization_barrier(narrow.reshape(devices, 2, local_src, receivers))
+        pieces = [
+            narrow.reshape(devices, 2 * shares, rows, receivers),
+            marked.reshape(devices, 1, rows, receivers),
+        ]
+        arrived = exchange(jnp.concatenate(pieces, axis=1))
+        halves = [arrived[:, 2 * shares]]
+        if shares == 2:
+            own, other = halves[0], lax.ppermute(halves[0], "freq", [(i, i ^ 1) for i in range(devices)])
+            halves = [jnp.minimum(own, other), jnp.maximum(own, other) - MARK]
+        return by_part(arrived[:, : 2 * shares]), jnp.stack(halves, axis=1).reshape(SOURCES, receivers)
 
     def to_traces(returned):
         pieces = returned.reshape(2, devices, local_src, receivers).swapaxes(0, 1)
@@ -281,11 +331,10 @@
     narrow, spectra, start, table, operator, recorded, radius = forward(
         start_field.reshape(rows, NT), table, block_index, multiples[0], recorded.reshape(-1, 2 * BS), radius
     )
-    arrived = to_owners(narrow, radius)
-    radius = arrived[2 * SOURCES :]
-    (returned,) = owner(arrived[: 2 * SOURCES], operator, recorded, radius, False)
+    arrived, radius = to_owners_with_radius(narrow, radius)
+    returned = smooth_sources(first_owner(arrived, operator, recorded), radius)
     field, narrow = middle(start, to_traces(returned), spectra, table)
-    returned, residual = owner(to_owners(narrow), operator, recorded, radius, True)
+    returned, residual = last_owner(to_owners(narrow), operator, recorded, radius)
     field = final(field, to_traces(returned), table)
     return field.reshape(local_src, receivers, NT), residual.reshape(1, receivers, NB, 2 * BS)
 

time: 87.2 us -> 85.5 us (0.981)
  blocking collectives: 70.5 us -> 68.1 us
    all_to_all x4, blocking collectives: 70.5 us -> 68.1 us  [exchange(): lax.all_to_all(pieces, 'freq', split_axis=0, concat_axis=0, tiled=True)]
    pallas_call x2 -> x3, Pallas kernels: 2.61 us -> 2.71 us  [the longest x1 1.31 us: last_owner(): pl.pallas_call(last_owner_kernel, in_specs=[VMEM] * 4, out_specs=[VMEM, A...]
  transfers between devices with their start and end apart: 0 -> 1, of which waited for: 0 -> 1; matrix products, arithmetic and copies ran while one was open for 0% -> 0% of each run, Pallas kernels for 0% -> 1%
where the time goes in v4:
time: 85.5 us; the launch traced here: 85.2 us
  blocking collectives  68.1 us (80%)
  Pallas kernels  15.2 us (18%)
    all_to_all x4, blocking collectives, exchange(): lax.all_to_all(pieces, 'freq', split_axis=0, concat_axis=0, tiled=True)  68.1 us
    pallas_call x1, Pallas kernels, final(): pl.pallas_call(final_kernel, in_specs=[VMEM] * 3, out_specs=ANY, out_shap...  4.96 us
    pallas_call x1, Pallas kernels, forward(): pl.pallas_call(forward_kernel, in_specs=[ANY] * 6, out_specs=[VMEM] * 7,...  4.11 us
    pallas_call x1, Pallas kernels, middle(): pl.pallas_call(lambda *refs: middle_kernel(*refs, step=step), in_specs=[V...  3.42 us
  transfers between devices with their start and end apart: 1, of which 1 were waited for; matrix products, arithmetic and copies ran while one was open for 0% of the time, Pallas kernels for 1%

profile of v4, /device:TPU:0, one launch (start us, length us, event | category | flops | bytes accessed | tf_op | source)
XLA Modules:
  0.0 85.2 jit_solution(17778402544484950721)
XLA Ops:
  0.6 4.1 %forward_dft.1 = (bf16[32,6144]{1,0:T(8,128)(2,1)S(1)}, f32[32,6144]{1,0:T(8,128)S(1)}, bf16[6144,512]{1,0:T(8,128)(2,1)S(1)}, bf16[64,512]{1,0:T(8,128)(2,1)S(1...) custom-call(bf16[6144,512]{1,0:T(8,128)(2,1)} %bitcast.57, ...), custom_call_target="tpu_custom_call" | custom-call | tf_op jit(solution)/shard_map/forward_dft/pallas_call | solution.py:119
  4.8 0.1 bitcast_add_fusion
  4.9 0.1 pad_maximum_fusion
  5.0 21.0 %all_to_all.20 = bf16[16,5,8,384]{3,2,1,0:T(8,128)(2,1)S(1)} all-to-all(bf16[16,5,8,384]{3,2,1,0:T(8,128)(2,1)S(1)} %pad_maximum_fusion), channel_id=1, replica_groups=mesh['grp'=2,'freq'=16] {'freq'}, dimensions={0} | all-to-all | bytes 983040 | tf_op jit(solution)/shard_map/all_to_all | solution.py:295
  25.9 0.2 collective-permute-start
  26.2 0.8 owner_products.1.backward_ref
  27.0 0.3 collective-permute-done
  27.4 0.6 smooth_sources.1
  28.1 16.1 %all_to_all.21 = bf16[16,2,16,384]{3,2,1,0:T(8,128)(2,1)S(1)} all-to-all(bf16[16,2,16,384]{3,2,1,0:T(8,128)(2,1)S(1)} %bitcast.58), channel_id=1, replica_groups=mesh['grp'=2,'freq'=16] {'freq'}, dimensions={0} | all-to-all | bytes 786432 | tf_op jit(solution)/shard_map/all_to_all | solution.py:295
  44.2 0.1 copy.23
  44.3 3.4 %update_and_forward.1 = (f32[6144,512]{1,0:T(8,128)S(1)}, bf16[32,6144]{1,0:T(8,128)(2,1)S(1)}) custom-call(bf16[6144,512]{1,0:T(8,128)(2,1)S(1)} %get-tuple-element.13.refs_0_, bf16[32,6144]{1,0:T(8,128)(2,1)S(1)} %bitcast.48, f32[32,6144]{1,0:T(8,128)S(1)} %get-tuple-element.18.refs_2_, bf16[64,512]{1,0:T(8,128)(2,1)S(1)} %get-tuple-element.19.refs_3_.table_ref), custom_call_target="tpu_custom_call" | custom-call | tf_op jit(solution)/shard_map/update_and_forward/pallas_call | solution.py:166
  47.7 15.5 %all_to_all.22 = bf16[16,2,16,384]{3,2,1,0:T(8,128)(2,1)S(1)} all-to-all(bf16[16,2,16,384]{3,2,1,0:T(8,128)(2,1)S(1)} %bitcast.60), channel_id=1, replica_groups=mesh['grp'=2,'freq'=16] {'freq'}, dimensions={0} | all-to-all | bytes 786432 | tf_op jit(solution)/shard_map/all_to_all | solution.py:295
  63.3 1.3 %owner_step.1 = (bf16[512,384]{1,0:T(8,128)(2,1)S(1)}, f32[1536,128]{1,0:T(8,128)}) custom-call(bf16[512,384]{1,0:T(8,128)(2,1)S(1)} %bitcast.51, bf16[512,512]{1,0:T(8,128)(2,1)S(1)} %get-tuple-element.16.operator_ref, f32[384,512]{1,0:T(8,128)S(1)} %get-tuple-element.17.recorded_ref, bf16[256,384]{1,0:T(8,128)(2,1)S(1)} %bitcast.47), custom_call_target="tpu_custom_call" | custom-call | tf_op jit(solution)/shard_map/owner_step/pallas_call | solution.py:280
  64.7 15.5 %all_to_all.23 = bf16[16,2,16,384]{3,2,1,0:T(8,128)(2,1)S(1)} all-to-all(bf16[16,2,16,384]{3,2,1,0:T(8,128)(2,1)S(1)} %bitcast.62), channel_id=1, replica_groups=mesh['grp'=2,'freq'=16] {'freq'}, dimensions={0} | all-to-all | bytes 786432 | tf_op jit(solution)/shard_map/all_to_all | solution.py:295
  80.2 0.1 copy.25
  80.3 5.0 %last_update.1 = f32[6144,512]{1,0:T(8,128)} custom-call(f32[6144,512]{1,0:T(8,128)S(1)} %get-tuple-element.20.field_ref, bf16[32,6144]{1,0:T(8,128)(2,1)S(1)} %bitcast.52, bf16[64,512]{1,0:T(8,128)(2,1)S(1)} %get-tuple-element.19.refs_3_.table_ref), custom_call_target="tpu_custom_call" | custom-call | tf_op jit(solution)/shard_map/last_update/pallas_call | solution.py:198
  (13 shorter events, 0.4 us)
Async XLA Ops:
  25.9 1.4 %collective-permute-start = (bf16[16,8,384]{2,1,0:T(8,128)(2,1)S(1)}, bf16[16,8,384]{2,1,0:T(8,128)(2,1)S(1)}, u32[]{:S(2)}, u32[]{:S(2)}) collective-permute-start(bf16[16,8,384]{2,1,0:T(8,128)(2,1)S(1)} %slice_bitcast_fusion), channel_id=1, source_target_pairs={{0,1},{1,0},{2,3},{3,2},{4,5},{5,4},{6,7},{7,6},{8,9},{9,8},{10,11... | collective-permute-start | bytes 294920 | tf_op jit(solution)/shard_map/ppermute | solution.py:323

commit v5 on v4

--- a/solution.py
+++ b/solution.py
@@ -15,6 +15,7 @@
 RADIUS = 4
 STEP = 0.5
 MARK = 8
+RANKS = (9, 11, 7, 3, 1, 4, 13, 8, 2, 5, 6, 12, 10, 0, 15, 14)
 SHRINKAGE = 0.05
 SOURCES = NB * BS
 WIDE = NB * 2 * BS
@@ -23,16 +24,30 @@
 ANY = pl.BlockSpec(memory_space=pl.ANY)
 
 
-def split_table(freq_count):
-    phases = np.arange(NT)[:, None] * (np.arange(freq_count) + 1)[None, :] % NT
+def ranking(devices, local_src):
+    fits = devices == len(RANKS) and local_src % 16 == 0 and BS % local_src == 0
+    return list(RANKS) if fits else list(range(devices))
+
+
+def split_table(ranks):
+    phases = np.arange(NT)[:, None] * (np.array(ranks) + 1)[None, :] % NT
     angles = phases * (2.0 * math.pi / NT)
-    table = np.stack([np.cos(angles), -np.sin(angles)], axis=-1).reshape(NT, 2 * freq_count) / math.sqrt(NT)
+    table = np.stack([np.cos(angles), -np.sin(angles)], axis=-1).reshape(NT, 2 * len(ranks)) / math.sqrt(NT)
     table = table.T.astype(np.float32)
     upper = table.astype(jnp.bfloat16)
     lower = (table - upper.astype(np.float32)).astype(jnp.bfloat16)
     return np.concatenate([upper, lower], axis=0)
 
 
+def row_places(ranks):
+    return np.arange(NB, dtype=np.int32) if ranks == sorted(ranks) else np.argsort(ranks).astype(np.int32)
+
+
+def distances(ranks, local_src):
+    sources = (np.array(ranks)[:, None] * local_src + np.arange(local_src)).reshape(-1)
+    return np.abs(sources[:, None] - sources[None, :]).astype(np.float32)
+
+
 def contract(a, b, dims):
     return lax.dot_general(a, b, ((dims[:1], dims[1:]), ((), ())), preferred_element_type=jnp.float32)
 
@@ -55,21 +70,26 @@
     return [slice(low, high) for low, high in zip(bounds[:-1], bounds[1:])]
 
 
-def build_operator(index_ref, multiples_ref, operator_ref):
+def build_operator(index_ref, places_ref, multiples_ref, operator_ref):
     operator_ref[...] = jnp.zeros_like(operator_ref)
+    runs = places_ref.shape[0] // NB
+    length = BS // runs
     for block in range(NB):
         columns = slice(block * 2 * BS, (block + 1) * 2 * BS)
         for band in range(BANDS):
-            first = pl.multiple_of(index_ref[block, band] * BS, BS)
             pair = multiples_ref[block, band]
-            operator_ref[pl.ds(first, BS), columns] = pair
-            operator_ref[pl.ds(SOURCES + first, BS), columns] = jnp.concatenate([-pair[:, BS:], pair[:, :BS]], axis=1)
+            turned = jnp.concatenate([-pair[:, BS:], pair[:, :BS]], axis=1)
+            for run in range(runs):
+                first = pl.multiple_of(places_ref[index_ref[block, band] * runs + run] * length, length)
+                part = slice(run * length, (run + 1) * length)
+                operator_ref[pl.ds(first, length), columns] = pair[part]
+                operator_ref[pl.ds(SOURCES + first, length), columns] = turned[part]
 
 
 def forward_kernel(
-    field_hbm, table_hbm, index_hbm, multiples_hbm, recorded_hbm, radius_hbm,
-    narrow_ref, spectra_ref, field_ref, table_ref, operator_ref, recorded_ref, radius_ref,
-    index, multiples, loaded, unpacked, radius, sems, field_sems,
+    field_hbm, table_hbm, index_hbm, places_hbm, multiples_hbm, recorded_hbm, radius_hbm, distance_hbm,
+    narrow_ref, spectra_ref, field_ref, table_ref, operator_ref, recorded_ref, radius_ref, distance_ref,
+    index, places, multiples, loaded, unpacked, radius, sems, field_sems, *, halves,
 ):
     receivers = recorded_ref.shape[0]
     count, rows = spectra_ref.shape
@@ -80,6 +100,8 @@
         pltpu.make_async_copy(multiples_hbm, multiples, sems.at[2]),
         pltpu.make_async_copy(recorded_hbm, loaded, sems.at[3]),
         pltpu.make_async_copy(radius_hbm, radius, sems.at[4]),
+        pltpu.make_async_copy(places_hbm, places, sems.at[5]),
+        pltpu.make_async_copy(distance_hbm, distance_ref, sems.at[6]),
     ]
     large = []
     for i, part in enumerate(parts):
@@ -99,7 +121,8 @@
     transform(0)
     small[1].wait()
     small[2].wait()
-    build_operator(index, multiples, operator_ref)
+    small[5].wait()
+    build_operator(index, places, multiples, operator_ref)
     for i in range(1, len(parts) // 2):
         transform(i)
     small[3].wait()
@@ -107,19 +130,26 @@
     for block in range(NB):
         recorded_ref[:, block * 2 * BS : (block + 1) * 2 * BS] = unpacked[pl.ds(block, receivers, stride=NB), :]
     small[4].wait()
-    radius_ref[...] = radius[...].astype(jnp.float32).astype(jnp.bfloat16)
+    shares, amount = max(halves) + 1, radius_ref.shape[1]
+    for share in range(shares):
+        rows_sent = radius[share * amount : (share + 1) * amount].astype(jnp.float32) + MARK * share
+        for rank, half in enumerate(halves):
+            if half == share:
+                radius_ref[rank] = rows_sent.astype(jnp.bfloat16)
     for i in range(max(1, len(parts) // 2), len(parts)):
         transform(i)
-
-
-def forward(field, table, block_index, multiples, recorded, radius):
+    small[6].wait()
+
+
+def forward(field, table, block_index, places, multiples, recorded, radius, distance, halves):
     rows, receivers = field.shape[0], radius.shape[1]
     count = table.shape[0] // 2
-    arguments = (field, table, block_index, multiples, recorded, radius)
-    return pl.pallas_call(
-        forward_kernel,
-        in_specs=[ANY] * 6,
-        out_specs=[VMEM] * 7,
+    arguments = (field, table, block_index, places, multiples, recorded, radius, distance)
+    sent = (len(halves), radius.shape[0] // (max(halves) + 1), receivers)
+    return pl.pallas_call(
+        lambda *refs: forward_kernel(*refs, halves=halves),
+        in_specs=[ANY] * 8,
+        out_specs=[VMEM] * 8,
         out_shape=[
             jax.ShapeDtypeStruct((count, rows), jnp.bfloat16),
             pltpu.VMEM((count, rows), jnp.float32),
@@ -127,15 +157,17 @@
             pltpu.VMEM(table.shape, jnp.bfloat16),
             pltpu.VMEM((2 * SOURCES, WIDE), jnp.bfloat16),
             pltpu.VMEM((receivers, WIDE), jnp.float32),
-            jax.ShapeDtypeStruct(radius.shape, jnp.bfloat16),
+            jax.ShapeDtypeStruct(sent, jnp.bfloat16),
+            pltpu.VMEM(distance.shape, jnp.float32),
         ],
         scratch_shapes=[
             pltpu.SMEM((NB, BANDS), jnp.int32),
+            pltpu.SMEM(places.shape, jnp.int32),
             pltpu.VMEM((NB, BANDS, BS, 2 * BS), jnp.bfloat16),
             pltpu.VMEM((receivers * NB, 2 * BS), jnp.bfloat16),
             pltpu.VMEM((receivers * NB, 2 * BS), jnp.float32),
             pltpu.VMEM(radius.shape, jnp.int32),
-            pltpu.SemaphoreType.DMA((5,)),
+            pltpu.SemaphoreType.DMA((7,)),
             pltpu.SemaphoreType.DMA((len(chunks(rows)),)),
         ],
         compiler_params=params(16),
@@ -206,14 +238,11 @@
     )(field, returned, table)
 
 
-def smooth(backward, radius):
+def smooth(backward, radius, distance):
     sources, receivers = radius.shape
     rows = jnp.concatenate([backward[:sources], backward[sources:]], axis=1)
     narrow = rows.astype(jnp.bfloat16)
     radius = jnp.concatenate([radius, radius], axis=1)
-    distance = jnp.abs(
-        lax.broadcasted_iota(jnp.int32, (sources, sources), 0) - lax.broadcasted_iota(jnp.int32, (sources, sources), 1)
-    )
     summed = rows
     for width in range(1, RADIUS + 1):
         band = jnp.where(distance <= width, 1.0, 0.0).astype(jnp.bfloat16)
@@ -232,12 +261,12 @@
     _, backward_ref[...] = adjoint(arrived_ref, operator_ref, recorded_ref)
 
 
-def smooth_kernel(backward_ref, radius_ref, returned_ref):
-    returned_ref[...] = smooth(backward_ref[...], radius_ref[...].astype(jnp.float32))
+def smooth_kernel(backward_ref, radius_ref, distance_ref, returned_ref):
+    returned_ref[...] = smooth(backward_ref[...], radius_ref[...].astype(jnp.float32), distance_ref[...])
 
 
 def last_owner_kernel(
-    arrived_ref, operator_ref, recorded_ref, radius_ref, returned_ref, residual_hbm, interleaved, sem
+    arrived_ref, operator_ref, recorded_ref, radius_ref, distance_ref, returned_ref, residual_hbm, interleaved, sem
 ):
     residual, backward = adjoint(arrived_ref, operator_ref, recorded_ref)
     for block in range(NB):
@@ -245,7 +274,7 @@
         interleaved[rows, :] = residual[:, block * 2 * BS : (block + 1) * 2 * BS]
     copy = pltpu.make_async_copy(interleaved, residual_hbm, sem)
     copy.start()
-    returned_ref[...] = smooth(backward, radius_ref[...].astype(jnp.float32))
+    returned_ref[...] = smooth(backward, radius_ref[...].astype(jnp.float32), distance_ref[...])
     copy.wait()
 
 
@@ -264,22 +293,22 @@
     )(arrived, operator, recorded)
 
 
-def smooth_sources(backward, radius):
+def smooth_sources(backward, radius, distance):
     return pl.pallas_call(
         smooth_kernel,
-        in_specs=[VMEM] * 2,
+        in_specs=[VMEM] * 3,
         out_specs=VMEM,
         out_shape=jax.ShapeDtypeStruct(backward.shape, jnp.bfloat16),
         compiler_params=params(16),
         name="smooth_sources",
-    )(backward, radius)
-
-
-def last_owner(arrived, operator, recorded, radius):
+    )(backward, radius, distance)
+
+
+def last_owner(arrived, operator, recorded, radius, distance):
     receivers = arrived.shape[1]
     return pl.pallas_call(
         last_owner_kernel,
-        in_specs=[VMEM] * 4,
+        in_specs=[VMEM] * 5,
         out_specs=[VMEM, ANY],
         out_shape=[
             jax.ShapeDtypeStruct((2 * SOURCES, receivers), jnp.bfloat16),
@@ -288,18 +317,20 @@
         scratch_shapes=[pltpu.VMEM((receivers * NB, 2 * BS), jnp.float32), pltpu.SemaphoreType.DMA(())],
         compiler_params=params(16),
         name="owner_step",
-    )(arrived, operator, recorded, radius)
-
-
-def exchange(pieces):
-    return lax.all_to_all(pieces, "freq", split_axis=0, concat_axis=0, tiled=True)
+    )(arrived, operator, recorded, radius, distance)
 
 
 def on_device(start_field, recorded, multiples, block_index, radius):
     devices = lax.axis_size("freq")
     local_src, receivers, _ = start_field.shape
     rows = local_src * receivers
-    table = jnp.asarray(split_table(devices))
+    ranks = ranking(devices, local_src)
+    places = row_places(ranks)
+    shares = 2 if devices % 2 == 0 and local_src % 2 == 0 else 1
+    table = jnp.asarray(split_table(ranks))
+
+    def exchange(pieces):
+        return lax.all_to_all(pieces, "freq", split_axis=0, concat_axis=0, tiled=True, axis_index_groups=[ranks])
 
     def by_part(arrived):
         return arrived.reshape(devices, 2, local_src, receivers).swapaxes(0, 1).reshape(2 * SOURCES, receivers)
@@ -308,14 +339,11 @@
         return by_part(exchange(narrow.reshape(devices, 2, local_src, receivers)))
 
     def to_owners_with_radius(narrow, radius):
-        shares = 2 if devices % 2 == 0 and local_src % 2 == 0 else 1
         rows = local_src // shares
-        marked = radius.reshape(shares, rows, receivers) + MARK * jnp.arange(shares, dtype=radius.dtype)[:, None, None]
-        marked = jnp.broadcast_to(marked, (devices // shares, shares, rows, receivers))
         narrow = lax.optimization_barrier(narrow.reshape(devices, 2, local_src, receivers))
         pieces = [
             narrow.reshape(devices, 2 * shares, rows, receivers),
-            marked.reshape(devices, 1, rows, receivers),
+            radius.reshape(devices, 1, rows, receivers),
         ]
         arrived = exchange(jnp.concatenate(pieces, axis=1))
         halves = [arrived[:, 2 * shares]]
@@ -328,13 +356,21 @@
         pieces = returned.reshape(2, devices, local_src, receivers).swapaxes(0, 1)
         return exchange(pieces).reshape(2 * devices, rows)
 
-    narrow, spectra, start, table, operator, recorded, radius = forward(
-        start_field.reshape(rows, NT), table, block_index, multiples[0], recorded.reshape(-1, 2 * BS), radius
+    narrow, spectra, start, table, operator, recorded, radius, distance = forward(
+        start_field.reshape(rows, NT),
+        table,
+        block_index,
+        jnp.asarray(places),
+        multiples[0],
+        recorded.reshape(-1, 2 * BS),
+        radius,
+        jnp.asarray(distances(ranks, local_src)),
+        [rank % shares for rank in ranks],
     )
     arrived, radius = to_owners_with_radius(narrow, radius)
-    returned = smooth_sources(first_owner(arrived, operator, recorded), radius)
+    returned = smooth_sources(first_owner(arrived, operator, recorded), radius, distance)
     field, narrow = middle(start, to_traces(returned), spectra, table)
-    returned, residual = last_owner(to_owners(narrow), operator, recorded, radius)
+    returned, residual = last_owner(to_owners(narrow), operator, recorded, radius, distance)
     field = final(field, to_traces(returned), table)
     return field.reshape(local_src, receivers, NT), residual.reshape(1, receivers, NB, 2 * BS)
 

time: 85.5 us -> 79.1 us (0.925)
  blocking collectives: 68.1 us -> 61.7 us
    all_to_all x4, blocking collectives: 68.1 us -> 61.7 us  [exchange(): lax.all_to_all(pieces, 'freq', split_axis=0, concat_axis=0, tiled=True, a...]
where the time goes in v5:
time: 79.1 us; the launch traced here: 78.8 us
  blocking collectives  61.7 us (78%)
  Pallas kernels  15.3 us (19%)
    all_to_all x4, blocking collectives, exchange(): lax.all_to_all(pieces, 'freq', split_axis=0, concat_axis=0, tiled=True, a...  61.7 us
    pallas_call x1, Pallas kernels, final(): pl.pallas_call(final_kernel, in_specs=[VMEM] * 3, out_specs=ANY, out_shap...  4.97 us
    pallas_call x1, Pallas kernels, forward(): pl.pallas_call(lambda *refs: forward_kernel(*refs, halves=halves), in_spe...  4.25 us
    pallas_call x1, Pallas kernels, middle(): pl.pallas_call(lambda *refs: middle_kernel(*refs, step=step), in_specs=[V...  3.38 us
  transfers between devices with their start and end apart: 1, of which 1 were waited for; matrix products, arithmetic and copies ran while one was open for 0% of the time, Pallas kernels for 1%

profile of v5, /device:TPU:0, one launch (start us, length us, event | category | flops | bytes accessed | tf_op | source)
XLA Modules:
  0.0 78.8 jit_solution(1212462006289302469)
XLA Ops:
  0.6 4.3 %forward_dft.1 = (bf16[32,6144]{1,0:T(8,128)(2,1)S(1)}, f32[32,6144]{1,0:T(8,128)S(1)}, bf16[6144,512]{1,0:T(8,128)(2,1)S(1)}, bf16[64,512]{1,0:T(8,128)(2,1)S(1...) custom-call(bf16[6144,512]{1,0:T(8,128)(2,1)} %bitcast.58, ...), custom_call_target="tpu_custom_call" | custom-call | tf_op jit(solution)/shard_map/forward_dft/pallas_call | solution.py:149
  4.9 0.1 pad_maximum_fusion
  5.0 19.1 %all_to_all.20 = bf16[16,5,8,384]{3,2,1,0:T(8,128)(2,1)S(1)} all-to-all(bf16[16,5,8,384]{3,2,1,0:T(8,128)(2,1)S(1)} %pad_maximum_fusion), channel_id=1, replica_groups={{9,11,7,3,1,4,13,8,2,5,6,12,10,0,15,14},{25,27,23,19,17,20,29,24,18,21,..., dimensions={0} | all-to-all | bytes 983040 | tf_op jit(solution)/shard_map/all_to_all | solution.py:333
  24.1 0.1 collective-permute-start
  24.3 0.8 owner_products.1.backward_ref
  25.1 0.4 collective-permute-done
  25.6 0.6 smooth_sources.1
  26.3 14.8 %all_to_all.21 = bf16[16,2,16,384]{3,2,1,0:T(8,128)(2,1)S(1)} all-to-all(bf16[16,2,16,384]{3,2,1,0:T(8,128)(2,1)S(1)} %bitcast.59), channel_id=1, replica_groups={{9,11,7,3,1,4,13,8,2,5,6,12,10,0,15,14},{25,27,23,19,17,20,29,24,18,21,..., dimensions={0} | all-to-all | bytes 786432 | tf_op jit(solution)/shard_map/all_to_all | solution.py:333
  41.1 0.1 copy.27
  41.2 3.4 %update_and_forward.1 = (f32[6144,512]{1,0:T(8,128)S(1)}, bf16[32,6144]{1,0:T(8,128)(2,1)S(1)}) custom-call(bf16[6144,512]{1,0:T(8,128)(2,1)S(1)} %get-tuple-element.14.refs_0_, bf16[32,6144]{1,0:T(8,128)(2,1)S(1)} %bitcast.48, f32[32,6144]{1,0:T(8,128)S(1)} %get-tuple-element.20.refs_2_, bf16[64,512]{1,0:T(8,128)(2,1)S(1)} %get-tuple-element.21.refs_3_.table_ref), custom_call_target="tpu_custom_call" | custom-call | tf_op jit(solution)/shard_map/update_and_forward/pallas_call | solution.py:198
  44.6 13.8 %all_to_all.22 = bf16[16,2,16,384]{3,2,1,0:T(8,128)(2,1)S(1)} all-to-all(bf16[16,2,16,384]{3,2,1,0:T(8,128)(2,1)S(1)} %bitcast.61), channel_id=1, replica_groups={{9,11,7,3,1,4,13,8,2,5,6,12,10,0,15,14},{25,27,23,19,17,20,29,24,18,21,..., dimensions={0} | all-to-all | bytes 786432 | tf_op jit(solution)/shard_map/all_to_all | solution.py:333
  58.5 1.3 %owner_step.1 = (bf16[512,384]{1,0:T(8,128)(2,1)S(1)}, f32[1536,128]{1,0:T(8,128)}) custom-call(bf16[512,384]{1,0:T(8,128)(2,1)S(1)} %bitcast.51, bf16[512,512]{1,0:T(8,128)(2,1)S(1)} %get-tuple-element.17.operator_ref, f32[384,512]{1,0:T(8,128)S(1)} %get-tuple-element.18.recorded_ref, bf16[256,384]{1,0:T(8,128)(2,1)S(1)} %bitcast.47, ...), custom_call_target="tpu_custom_call" | custom-call | tf_op jit(solution)/shard_map/owner_step/pallas_call | solution.py:309
  59.9 13.9 %all_to_all.23 = bf16[16,2,16,384]{3,2,1,0:T(8,128)(2,1)S(1)} all-to-all(bf16[16,2,16,384]{3,2,1,0:T(8,128)(2,1)S(1)} %bitcast.63), channel_id=1, replica_groups={{9,11,7,3,1,4,13,8,2,5,6,12,10,0,15,14},{25,27,23,19,17,20,29,24,18,21,..., dimensions={0} | all-to-all | bytes 786432 | tf_op jit(solution)/shard_map/all_to_all | solution.py:333
  73.8 0.1 copy.29
  73.9 5.0 %last_update.1 = f32[6144,512]{1,0:T(8,128)} custom-call(f32[6144,512]{1,0:T(8,128)S(1)} %get-tuple-element.22.field_ref, bf16[32,6144]{1,0:T(8,128)(2,1)S(1)} %bitcast.52, bf16[64,512]{1,0:T(8,128)(2,1)S(1)} %get-tuple-element.21.refs_3_.table_ref), custom_call_target="tpu_custom_call" | custom-call | tf_op jit(solution)/shard_map/last_update/pallas_call | solution.py:230
  (11 shorter events, 0.4 us)
Async XLA Ops:
  24.1 1.4 %collective-permute-start = (bf16[16,8,384]{2,1,0:T(8,128)(2,1)S(1)}, bf16[16,8,384]{2,1,0:T(8,128)(2,1)S(1)}, u32[]{:S(2)}, u32[]{:S(2)}) collective-permute-start(bf16[16,8,384]{2,1,0:T(8,128)(2,1)S(1)} %slice_bitcast_fusion), channel_id=1, source_target_pairs={{0,1},{1,0},{2,3},{3,2},{4,5},{5,4},{6,7},{7,6},{8,9},{9,8},{10,11... | collective-permute-start | bytes 294920 | tf_op jit(solution)/shard_map/ppermute | solution.py:351

commit v6 on v5

--- a/solution.py
+++ b/solution.py
@@ -15,7 +15,7 @@
 RADIUS = 4
 STEP = 0.5
 MARK = 8
-RANKS = (9, 11, 7, 3, 1, 4, 13, 8, 2, 5, 6, 12, 10, 0, 15, 14)
+RANKS = (11, 13, 15, 1, 3, 6, 5, 9, 2, 7, 4, 14, 8, 12, 10, 0)
 SHRINKAGE = 0.05
 SOURCES = NB * BS
 WIDE = NB * 2 * BS

time: 79.1 us -> 77.8 us (0.984)
  blocking collectives: 61.7 us -> 60.4 us
    all_to_all x4, blocking collectives: 61.7 us -> 60.4 us  [exchange(): lax.all_to_all(pieces, 'freq', split_axis=0, concat_axis=0, tiled=True, a...]
where the time goes in v6:
time: 77.8 us; the launch traced here: 77.5 us
  blocking collectives  60.4 us (78%)
  Pallas kernels  15.3 us (20%)
    all_to_all x4, blocking collectives, exchange(): lax.all_to_all(pieces, 'freq', split_axis=0, concat_axis=0, tiled=True, a...  60.4 us
    pallas_call x1, Pallas kernels, final(): pl.pallas_call(final_kernel, in_specs=[VMEM] * 3, out_specs=ANY, out_shap...  4.97 us
    pallas_call x1, Pallas kernels, forward(): pl.pallas_call(lambda *refs: forward_kernel(*refs, halves=halves), in_spe...  4.25 us
    pallas_call x1, Pallas kernels, middle(): pl.pallas_call(lambda *refs: middle_kernel(*refs, step=step), in_specs=[V...  3.38 us
  transfers between devices with their start and end apart: 1, of which 1 were waited for; matrix products, arithmetic and copies ran while one was open for 0% of the time, Pallas kernels for 1%

profile of v6, /device:TPU:0, one launch (start us, length us, event | category | flops | bytes accessed | tf_op | source)
XLA Modules:
  0.0 77.5 jit_solution(4511224718542572084)
XLA Ops:
  0.6 4.3 %forward_dft.1 = (bf16[32,6144]{1,0:T(8,128)(2,1)S(1)}, f32[32,6144]{1,0:T(8,128)S(1)}, bf16[6144,512]{1,0:T(8,128)(2,1)S(1)}, bf16[64,512]{1,0:T(8,128)(2,1)S(1...) custom-call(bf16[6144,512]{1,0:T(8,128)(2,1)} %bitcast.58, ...), custom_call_target="tpu_custom_call" | custom-call | tf_op jit(solution)/shard_map/forward_dft/pallas_call | solution.py:149
  4.9 0.1 pad_maximum_fusion
  5.0 18.7 %all_to_all.20 = bf16[16,5,8,384]{3,2,1,0:T(8,128)(2,1)S(1)} all-to-all(bf16[16,5,8,384]{3,2,1,0:T(8,128)(2,1)S(1)} %pad_maximum_fusion), channel_id=1, replica_groups={{11,13,15,1,3,6,5,9,2,7,4,14,8,12,10,0},{27,29,31,17,19,22,21,25,18,23,..., dimensions={0} | all-to-all | bytes 983040 | tf_op jit(solution)/shard_map/all_to_all | solution.py:333
  23.7 0.2 collective-permute-start
  24.0 0.8 %owner_products.1.backward_ref = f32[512,384]{1,0:T(8,128)S(1)} custom-call(bf16[512,384]{1,0:T(8,128)(2,1)S(1)} %bitcast.49, bf16[512,512]{1,0:T(8,128)(2,1)S(1)} %get-tuple-element.17.operator_ref, f32[384,512]{1,0:T(8,128)S(1)} %get-tuple-element.18.recorded_ref), custom_call_target="tpu_custom_call" | custom-call | flops 402653184 | bytes 1572864 | tf_op jit(solution)/shard_map/owner_products/pallas_call | solution.py:283
  24.8 0.3 collective-permute-done
  25.2 0.6 smooth_sources.1
  25.9 13.9 %all_to_all.21 = bf16[16,2,16,384]{3,2,1,0:T(8,128)(2,1)S(1)} all-to-all(bf16[16,2,16,384]{3,2,1,0:T(8,128)(2,1)S(1)} %bitcast.59), channel_id=1, replica_groups={{11,13,15,1,3,6,5,9,2,7,4,14,8,12,10,0},{27,29,31,17,19,22,21,25,18,23,..., dimensions={0} | all-to-all | bytes 786432 | tf_op jit(solution)/shard_map/all_to_all | solution.py:333
  39.8 0.1 copy.27
  39.9 3.4 %update_and_forward.1 = (f32[6144,512]{1,0:T(8,128)S(1)}, bf16[32,6144]{1,0:T(8,128)(2,1)S(1)}) custom-call(bf16[6144,512]{1,0:T(8,128)(2,1)S(1)} %get-tuple-element.14.refs_0_, bf16[32,6144]{1,0:T(8,128)(2,1)S(1)} %bitcast.48, f32[32,6144]{1,0:T(8,128)S(1)} %get-tuple-element.20.refs_2_, bf16[64,512]{1,0:T(8,128)(2,1)S(1)} %get-tuple-element.21.refs_3_.table_ref), custom_call_target="tpu_custom_call" | custom-call | tf_op jit(solution)/shard_map/update_and_forward/pallas_call | solution.py:198
  43.3 13.9 %all_to_all.22 = bf16[16,2,16,384]{3,2,1,0:T(8,128)(2,1)S(1)} all-to-all(bf16[16,2,16,384]{3,2,1,0:T(8,128)(2,1)S(1)} %bitcast.61), channel_id=1, replica_groups={{11,13,15,1,3,6,5,9,2,7,4,14,8,12,10,0},{27,29,31,17,19,22,21,25,18,23,..., dimensions={0} | all-to-all | bytes 786432 | tf_op jit(solution)/shard_map/all_to_all | solution.py:333
  57.2 1.3 %owner_step.1 = (bf16[512,384]{1,0:T(8,128)(2,1)S(1)}, f32[1536,128]{1,0:T(8,128)}) custom-call(bf16[512,384]{1,0:T(8,128)(2,1)S(1)} %bitcast.51, bf16[512,512]{1,0:T(8,128)(2,1)S(1)} %get-tuple-element.17.operator_ref, f32[384,512]{1,0:T(8,128)S(1)} %get-tuple-element.18.recorded_ref, bf16[256,384]{1,0:T(8,128)(2,1)S(1)} %bitcast.47, ...), custom_call_target="tpu_custom_call" | custom-call | tf_op jit(solution)/shard_map/owner_step/pallas_call | solution.py:309
  58.6 13.9 %all_to_all.23 = bf16[16,2,16,384]{3,2,1,0:T(8,128)(2,1)S(1)} all-to-all(bf16[16,2,16,384]{3,2,1,0:T(8,128)(2,1)S(1)} %bitcast.63), channel_id=1, replica_groups={{11,13,15,1,3,6,5,9,2,7,4,14,8,12,10,0},{27,29,31,17,19,22,21,25,18,23,..., dimensions={0} | all-to-all | bytes 786432 | tf_op jit(solution)/shard_map/all_to_all | solution.py:333
  72.5 0.1 copy.29
  72.6 5.0 %last_update.1 = f32[6144,512]{1,0:T(8,128)} custom-call(f32[6144,512]{1,0:T(8,128)S(1)} %get-tuple-element.22.field_ref, bf16[32,6144]{1,0:T(8,128)(2,1)S(1)} %bitcast.52, bf16[64,512]{1,0:T(8,128)(2,1)S(1)} %get-tuple-element.21.refs_3_.table_ref), custom_call_target="tpu_custom_call" | custom-call | tf_op jit(solution)/shard_map/last_update/pallas_call | solution.py:230
  (11 shorter events, 0.4 us)
Async XLA Ops:
  23.7 1.4 %collective-permute-start = (bf16[16,8,384]{2,1,0:T(8,128)(2,1)S(1)}, bf16[16,8,384]{2,1,0:T(8,128)(2,1)S(1)}, u32[]{:S(2)}, u32[]{:S(2)}) collective-permute-start(bf16[16,8,384]{2,1,0:T(8,128)(2,1)S(1)} %slice_bitcast_fusion), channel_id=1, source_target_pairs={{0,1},{1,0},{2,3},{3,2},{4,5},{5,4},{6,7},{7,6},{8,9},{9,8},{10,11... | collective-permute-start | bytes 294920 | tf_op jit(solution)/shard_map/ppermute | solution.py:351

commit v7 on v6

--- a/solution.py
+++ b/solution.py
@@ -238,7 +238,7 @@
     )(field, returned, table)
 
 
-def smooth(backward, radius, distance):
+def smooth(backward, radius, distance, returned_ref):
     sources, receivers = radius.shape
     rows = jnp.concatenate([backward[:sources], backward[sources:]], axis=1)
     narrow = rows.astype(jnp.bfloat16)
@@ -248,12 +248,22 @@
         band = jnp.where(distance <= width, 1.0, 0.0).astype(jnp.bfloat16)
         summed = jnp.where(radius >= width, contract(band, narrow, (1, 0)), summed)
     smoothed = (summed * (STEP / (2.0 * radius + 1.0))).astype(jnp.bfloat16)
-    return jnp.concatenate([smoothed[:, :receivers], smoothed[:, receivers:]], axis=0)
+    for part in range(2):
+        own = smoothed[:, part * receivers : (part + 1) * receivers]
+        if len(returned_ref.shape) == 4:
+            returned_ref[:, part] = own.reshape(returned_ref.shape[0], *returned_ref.shape[2:])
+        else:
+            returned_ref[part * sources : (part + 1) * sources] = own
 
 
 def adjoint(arrived_ref, operator_ref, recorded_ref):
     operator = operator_ref[...]
-    residual = recorded_ref[...] - contract(arrived_ref[...], operator, (0, 0))
+    if len(arrived_ref.shape) == 4:
+        parts = [arrived_ref[:, part].reshape(SOURCES, arrived_ref.shape[3]) for part in range(2)]
+        arrived = jnp.concatenate(parts, axis=0)
+    else:
+        arrived = arrived_ref[...]
+    residual = recorded_ref[...] - contract(arrived, operator, (0, 0))
     return residual, contract(operator, residual.astype(jnp.bfloat16), (1, 1))
 
 
@@ -261,8 +271,16 @@
     _, backward_ref[...] = adjoint(arrived_ref, operator_ref, recorded_ref)
 
 
-def smooth_kernel(backward_ref, radius_ref, distance_ref, returned_ref):
-    returned_ref[...] = smooth(backward_ref[...], radius_ref[...].astype(jnp.float32), distance_ref[...])
+def smooth_kernel(*refs):
+    backward_ref, *halves, distance_ref, returned_ref, radius_ref = refs
+    if len(halves) == 2:
+        own, other = (half[...].astype(jnp.float32) for half in halves)
+        both = jnp.stack([jnp.minimum(own, other), jnp.maximum(own, other) - MARK], axis=1)
+        radius = both.reshape(radius_ref.shape)
+    else:
+        radius = halves[0][...].astype(jnp.float32)
+    radius_ref[...] = radius
+    smooth(backward_ref[...], radius, distance_ref[...], returned_ref)
 
 
 def last_owner_kernel(
@@ -274,7 +292,7 @@
         interleaved[rows, :] = residual[:, block * 2 * BS : (block + 1) * 2 * BS]
     copy = pltpu.make_async_copy(interleaved, residual_hbm, sem)
     copy.start()
-    returned_ref[...] = smooth(backward, radius_ref[...].astype(jnp.float32), distance_ref[...])
+    smooth(backward, radius_ref[...], distance_ref[...], returned_ref)
     copy.wait()
 
 
@@ -293,25 +311,28 @@
     )(arrived, operator, recorded)
 
 
-def smooth_sources(backward, radius, distance):
+def smooth_sources(backward, radius, distance, shape):
     return pl.pallas_call(
         smooth_kernel,
-        in_specs=[VMEM] * 3,
-        out_specs=VMEM,
-        out_shape=jax.ShapeDtypeStruct(backward.shape, jnp.bfloat16),
+        in_specs=[VMEM] * (2 + len(radius)),
+        out_specs=[VMEM] * 2,
+        out_shape=[
+            jax.ShapeDtypeStruct(shape, jnp.bfloat16),
+            pltpu.VMEM((SOURCES, backward.shape[1]), jnp.float32),
+        ],
         compiler_params=params(16),
         name="smooth_sources",
-    )(backward, radius, distance)
-
-
-def last_owner(arrived, operator, recorded, radius, distance):
-    receivers = arrived.shape[1]
+    )(backward, *radius, distance)
+
+
+def last_owner(arrived, operator, recorded, radius, distance, shape):
+    receivers = recorded.shape[0]
     return pl.pallas_call(
         last_owner_kernel,
         in_specs=[VMEM] * 5,
         out_specs=[VMEM, ANY],
         out_shape=[
-            jax.ShapeDtypeStruct((2 * SOURCES, receivers), jnp.bfloat16),
+            jax.ShapeDtypeStruct(shape, jnp.bfloat16),
             pltpu.HBM((receivers * NB, 2 * BS), jnp.float32),
         ],
         scratch_shapes=[pltpu.VMEM((receivers * NB, 2 * BS), jnp.float32), pltpu.SemaphoreType.DMA(())],
@@ -326,6 +347,8 @@
     rows = local_src * receivers
     ranks = ranking(devices, local_src)
     places = row_places(ranks)
+    whole_tiles = local_src % 16 == 0
+    sent = (devices, 2, local_src, receivers) if whole_tiles else (2 * SOURCES, receivers)
     shares = 2 if devices % 2 == 0 and local_src % 2 == 0 else 1
     table = jnp.asarray(split_table(ranks))
 
@@ -336,7 +359,8 @@
         return arrived.reshape(devices, 2, local_src, receivers).swapaxes(0, 1).reshape(2 * SOURCES, receivers)
 
     def to_owners(narrow):
-        return by_part(exchange(narrow.reshape(devices, 2, local_src, receivers)))
+        arrived = exchange(narrow.reshape(devices, 2, local_src, receivers))
+        return arrived if whole_tiles else by_part(arrived)
 
     def to_owners_with_radius(narrow, radius):
         rows = local_src // shares
@@ -349,12 +373,16 @@
         halves = [arrived[:, 2 * shares]]
         if shares == 2:
             own, other = halves[0], lax.ppermute(halves[0], "freq", [(i, i ^ 1) for i in range(devices)])
+            if whole_tiles:
+                return by_part(arrived[:, : 2 * shares]), [own, other]
             halves = [jnp.minimum(own, other), jnp.maximum(own, other) - MARK]
-        return by_part(arrived[:, : 2 * shares]), jnp.stack(halves, axis=1).reshape(SOURCES, receivers)
+        radius = jnp.stack(halves, axis=1).reshape(SOURCES, receivers)
+        return by_part(arrived[:, : 2 * shares]), [radius]
 
     def to_traces(returned):
-        pieces = returned.reshape(2, devices, local_src, receivers).swapaxes(0, 1)
-        return exchange(pieces).reshape(2 * devices, rows)
+        if not whole_tiles:
+            returned = returned.reshape(2, devices, local_src, receivers).swapaxes(0, 1)
+        return exchange(returned).reshape(2 * devices, rows)
 
     narrow, spectra, start, table, operator, recorded, radius, distance = forward(
         start_field.reshape(rows, NT),
@@ -368,9 +396,9 @@
         [rank % shares for rank in ranks],
     )
     arrived, radius = to_owners_with_radius(narrow, radius)
-    returned = smooth_sources(first_owner(arrived, operator, recorded), radius, distance)
+    returned, radius = smooth_sources(first_owner(arrived, operator, recorded), radius, distance, sent)
     field, narrow = middle(start, to_traces(returned), spectra, table)
-    returned, residual = last_owner(to_owners(narrow), operator, recorded, radius, distance)
+    returned, residual = last_owner(to_owners(narrow), operator, recorded, radius, distance, sent)
     field = final(field, to_traces(returned), table)
     return field.reshape(local_src, receivers, NT), residual.reshape(1, receivers, NB, 2 * BS)
 

time: 77.8 us -> 77.6 us (level)
  no operation moved by 1% of the time
where the time goes in v7:
time: 77.6 us; the launch traced here: 77.3 us
  blocking collectives  60.4 us (78%)
  Pallas kernels  15.4 us (20%)
    all_to_all x4, blocking collectives, exchange(): lax.all_to_all(pieces, 'freq', split_axis=0, concat_axis=0, tiled=True, a...  60.4 us
    pallas_call x1, Pallas kernels, final(): pl.pallas_call(final_kernel, in_specs=[VMEM] * 3, out_specs=ANY, out_shap...  4.97 us
    pallas_call x1, Pallas kernels, forward(): pl.pallas_call(lambda *refs: forward_kernel(*refs, halves=halves), in_spe...  4.25 us
    pallas_call x1, Pallas kernels, middle(): pl.pallas_call(lambda *refs: middle_kernel(*refs, step=step), in_specs=[V...  3.38 us
  transfers between devices with their start and end apart: 1, of which 1 were waited for; matrix products, arithmetic and copies ran while one was open for 0% of the time, Pallas kernels for 1%

profile of v7, /device:TPU:0, one launch (start us, length us, event | category | flops | bytes accessed | tf_op | source)
XLA Modules:
  0.0 77.3 jit_solution(12196662435924707266)
XLA Ops:
  0.6 4.3 %forward_dft.1 = (bf16[32,6144]{1,0:T(8,128)(2,1)S(1)}, f32[32,6144]{1,0:T(8,128)S(1)}, bf16[6144,512]{1,0:T(8,128)(2,1)S(1)}, bf16[64,512]{1,0:T(8,128)(2,1)S(1...) custom-call(bf16[6144,512]{1,0:T(8,128)(2,1)} %bitcast.36, ...), custom_call_target="tpu_custom_call" | custom-call | tf_op jit(solution)/shard_map/forward_dft/pallas_call | solution.py:149
  4.9 0.1 pad_maximum_fusion
  5.0 18.7 %all_to_all.20 = bf16[16,5,8,384]{3,2,1,0:T(8,128)(2,1)S(1)} all-to-all(bf16[16,5,8,384]{3,2,1,0:T(8,128)(2,1)S(1)} %pad_maximum_fusion), channel_id=1, replica_groups={{11,13,15,1,3,6,5,9,2,7,4,14,8,12,10,0},{27,29,31,17,19,22,21,25,18,23,..., dimensions={0} | all-to-all | bytes 983040 | tf_op jit(solution)/shard_map/all_to_all | solution.py:356
  23.7 0.2 collective-permute-start
  24.0 0.8 %owner_products.1.refs_0_ = f32[512,384]{1,0:T(8,128)S(1)} custom-call(bf16[512,384]{1,0:T(8,128)(2,1)S(1)} %bitcast.30, bf16[512,512]{1,0:T(8,128)(2,1)S(1)} %get-tuple-element.19.operator_ref, f32[384,512]{1,0:T(8,128)S(1)} %get-tuple-element.20.recorded_ref), custom_call_target="tpu_custom_call" | custom-call | flops 402653184 | bytes 1572864 | tf_op jit(solution)/shard_map/owner_products/pallas_call | solution.py:301
  24.8 0.3 collective-permute-done.refs_2_
  25.1 0.6 smooth_sources.1
  25.8 13.9 %all_to_all.21 = bf16[16,2,16,384]{3,2,1,0:T(8,128)(2,1)S(1)} all-to-all(bf16[16,2,16,384]{3,2,1,0:T(8,128)(2,1)S(1)} %get-tuple-element.22), channel_id=1, replica_groups={{11,13,15,1,3,6,5,9,2,7,4,14,8,12,10,0},{27,29,31,17,19,22,21,25,18,23,..., dimensions={0} | all-to-all | bytes 786432 | tf_op jit(solution)/shard_map/all_to_all | solution.py:356
  39.6 0.1 copy.18
  39.7 3.4 %update_and_forward.1 = (f32[6144,512]{1,0:T(8,128)S(1)}, bf16[32,6144]{1,0:T(8,128)(2,1)S(1)}) custom-call(bf16[6144,512]{1,0:T(8,128)(2,1)S(1)} %get-tuple-element.16.refs_0_, bf16[32,6144]{1,0:T(8,128)(2,1)S(1)} %bitcast.29, f32[32,6144]{1,0:T(8,128)S(1)} %get-tuple-element.23.refs_2_, bf16[64,512]{1,0:T(8,128)(2,1)S(1)} %get-tuple-element.24.refs_3_.table_ref), custom_call_target="tpu_custom_call" | custom-call | tf_op jit(solution)/shard_map/update_and_forward/pallas_call | solution.py:198
  43.2 13.9 %all_to_all.22.arrived_ref = bf16[16,2,16,384]{3,2,1,0:T(8,128)(2,1)S(1)} all-to-all(bf16[16,2,16,384]{3,2,1,0:T(8,128)(2,1)S(1)} %bitcast.39), channel_id=1, replica_groups={{11,13,15,1,3,6,5,9,2,7,4,14,8,12,10,0},{27,29,31,17,19,22,21,25,18,23,..., dimensions={0} | all-to-all | bytes 786432 | tf_op jit(solution)/shard_map/all_to_all | solution.py:356
  57.1 1.3 %owner_step.1 = (bf16[16,2,16,384]{3,2,1,0:T(8,128)(2,1)S(1)}, f32[1536,128]{1,0:T(8,128)}) custom-call(bf16[16,2,16,384]{3,2,1,0:T(8,128)(2,1)S(1)} %all_to_all.22.arrived_ref, bf16[512,512]{1,0:T(8,128)(2,1)S(1)} %get-tuple-element.19.operator_ref, f32[384,512]{1,0:T(8,128)S(1)} %get-tuple-element.20.recorded_ref, ...), custom_call_target="tpu_custom_call" | custom-call | tf_op jit(solution)/shard_map/owner_step/pallas_call | solution.py:330
  58.4 13.9 %all_to_all.23 = bf16[16,2,16,384]{3,2,1,0:T(8,128)(2,1)S(1)} all-to-all(bf16[16,2,16,384]{3,2,1,0:T(8,128)(2,1)S(1)} %get-tuple-element.28), channel_id=1, replica_groups={{11,13,15,1,3,6,5,9,2,7,4,14,8,12,10,0},{27,29,31,17,19,22,21,25,18,23,..., dimensions={0} | all-to-all | bytes 786432 | tf_op jit(solution)/shard_map/all_to_all | solution.py:356
  72.3 0.1 copy.20
  72.4 5.0 %last_update.1 = f32[6144,512]{1,0:T(8,128)} custom-call(f32[6144,512]{1,0:T(8,128)S(1)} %get-tuple-element.25.field_ref, bf16[32,6144]{1,0:T(8,128)(2,1)S(1)} %bitcast.31, bf16[64,512]{1,0:T(8,128)(2,1)S(1)} %get-tuple-element.24.refs_3_.table_ref), custom_call_target="tpu_custom_call" | custom-call | tf_op jit(solution)/shard_map/last_update/pallas_call | solution.py:230
  (5 shorter events, 0.2 us)
Async XLA Ops:
  23.7 1.4 %collective-permute-start = (bf16[16,8,384]{2,1,0:T(8,128)(2,1)S(1)}, bf16[16,8,384]{2,1,0:T(8,128)(2,1)S(1)}, u32[]{:S(2)}, u32[]{:S(2)}) collective-permute-start(bf16[16,8,384]{2,1,0:T(8,128)(2,1)S(1)} %slice_bitcast_fusion.refs_1_), channel_id=1, source_target_pairs={{0,1},{1,0},{2,3},{3,2},{4,5},{5,4},{6,7},{7,6},{8,9},{9,8},{10,11... | collective-permute-start | bytes 294920 | tf_op jit(solution)/shard_map/ppermute | solution.py:375

commit v8 on v7

--- a/solution.py
+++ b/solution.py
@@ -89,9 +89,8 @@
 def forward_kernel(
     field_hbm, table_hbm, index_hbm, places_hbm, multiples_hbm, recorded_hbm, radius_hbm, distance_hbm,
     narrow_ref, spectra_ref, field_ref, table_ref, operator_ref, recorded_ref, radius_ref, distance_ref,
-    index, places, multiples, loaded, unpacked, radius, sems, field_sems, *, halves,
+    index, places, multiples, loaded, radius, sems, field_sems, *, halves,
 ):
-    receivers = recorded_ref.shape[0]
     count, rows = spectra_ref.shape
     parts = chunks(rows)
     small = [
@@ -126,9 +125,7 @@
     for i in range(1, len(parts) // 2):
         transform(i)
     small[3].wait()
-    unpacked[...] = loaded[...].astype(jnp.float32)
-    for block in range(NB):
-        recorded_ref[:, block * 2 * BS : (block + 1) * 2 * BS] = unpacked[pl.ds(block, receivers, stride=NB), :]
+    recorded_ref[...] = loaded[...].astype(jnp.float32)
     small[4].wait()
     shares, amount = max(halves) + 1, radius_ref.shape[1]
     for share in range(shares):
@@ -156,7 +153,7 @@
             pltpu.VMEM((rows, NT), jnp.bfloat16),
             pltpu.VMEM(table.shape, jnp.bfloat16),
             pltpu.VMEM((2 * SOURCES, WIDE), jnp.bfloat16),
-            pltpu.VMEM((receivers, WIDE), jnp.float32),
+            pltpu.VMEM((receivers * NB, 2 * BS), jnp.float32),
             jax.ShapeDtypeStruct(sent, jnp.bfloat16),
             pltpu.VMEM(distance.shape, jnp.float32),
         ],
@@ -165,7 +162,6 @@
             pltpu.SMEM(places.shape, jnp.int32),
             pltpu.VMEM((NB, BANDS, BS, 2 * BS), jnp.bfloat16),
             pltpu.VMEM((receivers * NB, 2 * BS), jnp.bfloat16),
-            pltpu.VMEM((receivers * NB, 2 * BS), jnp.float32),
             pltpu.VMEM(radius.shape, jnp.int32),
             pltpu.SemaphoreType.DMA((7,)),
             pltpu.SemaphoreType.DMA((len(chunks(rows)),)),
@@ -263,7 +259,9 @@
         arrived = jnp.concatenate(parts, axis=0)
     else:
         arrived = arrived_ref[...]
-    residual = recorded_ref[...] - contract(arrived, operator, (0, 0))
+    receivers = recorded_ref.shape[0] // NB
+    blocks = [recorded_ref[pl.ds(block, receivers, stride=NB), :] for block in range(NB)]
+    residual = jnp.concatenate(blocks, axis=1) - contract(arrived, operator, (0, 0))
     return residual, contract(operator, residual.astype(jnp.bfloat16), (1, 1))
 
 
@@ -297,7 +295,7 @@
 
 
 def first_owner(arrived, operator, recorded):
-    receivers = arrived.shape[1]
+    receivers = recorded.shape[0] // NB
     return pl.pallas_call(
         first_owner_kernel,
         in_specs=[VMEM] * 3,
@@ -326,7 +324,7 @@
 
 
 def last_owner(arrived, operator, recorded, radius, distance, shape):
-    receivers = recorded.shape[0]
+    receivers = recorded.shape[0] // NB
     return pl.pallas_call(
         last_owner_kernel,
         in_specs=[VMEM] * 5,

time: 77.6 us -> 77.5 us (level)
  no operation moved by 1% of the time
where the time goes in v8:
time: 77.5 us; the launch traced here: 77.2 us
  blocking collectives  60.4 us (78%)
  Pallas kernels  15.3 us (20%)
    all_to_all x4, blocking collectives, exchange(): lax.all_to_all(pieces, 'freq', split_axis=0, concat_axis=0, tiled=True, a...  60.4 us
    pallas_call x1, Pallas kernels, final(): pl.pallas_call(final_kernel, in_specs=[VMEM] * 3, out_specs=ANY, out_shap...  4.97 us
    pallas_call x1, Pallas kernels, forward(): pl.pallas_call(lambda *refs: forward_kernel(*refs, halves=halves), in_spe...  4.15 us
    pallas_call x1, Pallas kernels, middle(): pl.pallas_call(lambda *refs: middle_kernel(*refs, step=step), in_specs=[V...  3.38 us
  transfers between devices with their start and end apart: 1, of which 1 were waited for; matrix products, arithmetic and copies ran while one was open for 0% of the time, Pallas kernels for 1%

profile of v8, /device:TPU:0, one launch (start us, length us, event | category | flops | bytes accessed | tf_op | source)
XLA Modules:
  0.0 77.2 jit_solution(11253822458886550762)
XLA Ops:
  0.6 4.2 %forward_dft.1 = (bf16[32,6144]{1,0:T(8,128)(2,1)S(1)}, f32[32,6144]{1,0:T(8,128)S(1)}, bf16[6144,512]{1,0:T(8,128)(2,1)S(1)}, bf16[64,512]{1,0:T(8,128)(2,1)S(1...) custom-call(bf16[6144,512]{1,0:T(8,128)(2,1)} %bitcast.36, ...), custom_call_target="tpu_custom_call" | custom-call | tf_op jit(solution)/shard_map/forward_dft/pallas_call | solution.py:146
  4.8 0.1 pad_maximum_fusion
  4.9 18.7 %all_to_all.20 = bf16[16,5,8,384]{3,2,1,0:T(8,128)(2,1)S(1)} all-to-all(bf16[16,5,8,384]{3,2,1,0:T(8,128)(2,1)S(1)} %pad_maximum_fusion), channel_id=1, replica_groups={{11,13,15,1,3,6,5,9,2,7,4,14,8,12,10,0},{27,29,31,17,19,22,21,25,18,23,..., dimensions={0} | all-to-all | bytes 983040 | tf_op jit(solution)/shard_map/all_to_all | solution.py:354
  23.6 0.2 collective-permute-start
  23.9 0.8 %owner_products.1.refs_0_ = f32[512,384]{1,0:T(8,128)S(1)} custom-call(bf16[512,384]{1,0:T(8,128)(2,1)S(1)} %bitcast.30, bf16[512,512]{1,0:T(8,128)(2,1)S(1)} %get-tuple-element.19.operator_ref, f32[1536,128]{1,0:T(8,128)S(1)} %get-tuple-element.20.recorded_ref), custom_call_target="tpu_custom_call" | custom-call | flops 402653184 | bytes 1572864 | tf_op jit(solution)/shard_map/owner_products/pallas_call | solution.py:299
  24.7 0.3 collective-permute-done.refs_2_
  25.0 0.6 smooth_sources.1
  25.7 13.9 %all_to_all.21 = bf16[16,2,16,384]{3,2,1,0:T(8,128)(2,1)S(1)} all-to-all(bf16[16,2,16,384]{3,2,1,0:T(8,128)(2,1)S(1)} %get-tuple-element.22), channel_id=1, replica_groups={{11,13,15,1,3,6,5,9,2,7,4,14,8,12,10,0},{27,29,31,17,19,22,21,25,18,23,..., dimensions={0} | all-to-all | bytes 786432 | tf_op jit(solution)/shard_map/all_to_all | solution.py:354
  39.5 0.1 copy.18
  39.6 3.4 %update_and_forward.1 = (f32[6144,512]{1,0:T(8,128)S(1)}, bf16[32,6144]{1,0:T(8,128)(2,1)S(1)}) custom-call(bf16[6144,512]{1,0:T(8,128)(2,1)S(1)} %get-tuple-element.16.refs_0_, bf16[32,6144]{1,0:T(8,128)(2,1)S(1)} %bitcast.29, f32[32,6144]{1,0:T(8,128)S(1)} %get-tuple-element.23.refs_2_, bf16[64,512]{1,0:T(8,128)(2,1)S(1)} %get-tuple-element.24.refs_3_.table_ref), custom_call_target="tpu_custom_call" | custom-call | tf_op jit(solution)/shard_map/update_and_forward/pallas_call | solution.py:194
  43.1 13.9 %all_to_all.22.arrived_ref = bf16[16,2,16,384]{3,2,1,0:T(8,128)(2,1)S(1)} all-to-all(bf16[16,2,16,384]{3,2,1,0:T(8,128)(2,1)S(1)} %bitcast.39), channel_id=1, replica_groups={{11,13,15,1,3,6,5,9,2,7,4,14,8,12,10,0},{27,29,31,17,19,22,21,25,18,23,..., dimensions={0} | all-to-all | bytes 786432 | tf_op jit(solution)/shard_map/all_to_all | solution.py:354
  57.0 1.3 %owner_step.1 = (bf16[16,2,16,384]{3,2,1,0:T(8,128)(2,1)S(1)}, f32[1536,128]{1,0:T(8,128)}) custom-call(bf16[16,2,16,384]{3,2,1,0:T(8,128)(2,1)S(1)} %all_to_all.22.arrived_ref, bf16[512,512]{1,0:T(8,128)(2,1)S(1)} %get-tuple-element.19.operator_ref, f32[1536,128]{1,0:T(8,128)S(1)} %get-tuple-element.20.recorded_ref, ...), custom_call_target="tpu_custom_call" | custom-call | tf_op jit(solution)/shard_map/owner_step/pallas_call | solution.py:328
  58.3 13.9 %all_to_all.23 = bf16[16,2,16,384]{3,2,1,0:T(8,128)(2,1)S(1)} all-to-all(bf16[16,2,16,384]{3,2,1,0:T(8,128)(2,1)S(1)} %get-tuple-element.28), channel_id=1, replica_groups={{11,13,15,1,3,6,5,9,2,7,4,14,8,12,10,0},{27,29,31,17,19,22,21,25,18,23,..., dimensions={0} | all-to-all | bytes 786432 | tf_op jit(solution)/shard_map/all_to_all | solution.py:354
  72.2 0.1 copy.20
  72.3 5.0 %last_update.1 = f32[6144,512]{1,0:T(8,128)} custom-call(f32[6144,512]{1,0:T(8,128)S(1)} %get-tuple-element.25.field_ref, bf16[32,6144]{1,0:T(8,128)(2,1)S(1)} %bitcast.31, bf16[64,512]{1,0:T(8,128)(2,1)S(1)} %get-tuple-element.24.refs_3_.table_ref), custom_call_target="tpu_custom_call" | custom-call | tf_op jit(solution)/shard_map/last_update/pallas_call | solution.py:226
  (5 shorter events, 0.2 us)
Async XLA Ops:
  23.6 1.4 %collective-permute-start = (bf16[16,8,384]{2,1,0:T(8,128)(2,1)S(1)}, bf16[16,8,384]{2,1,0:T(8,128)(2,1)S(1)}, u32[]{:S(2)}, u32[]{:S(2)}) collective-permute-start(bf16[16,8,384]{2,1,0:T(8,128)(2,1)S(1)} %slice_bitcast_fusion.refs_1_), channel_id=1, source_target_pairs={{0,1},{1,0},{2,3},{3,2},{4,5},{5,4},{6,7},{7,6},{8,9},{9,8},{10,11... | collective-permute-start | bytes 294920 | tf_op jit(solution)/shard_map/ppermute | solution.py:373

commit v9 on v8

--- a/solution.py
+++ b/solution.py
@@ -66,7 +66,7 @@
 
 def chunks(rows):
     unit = rows // 128 // 6 * 128
-    bounds = [0, unit, 2 * unit, 4 * unit, rows] if unit else [0, rows]
+    bounds = [0, unit, 2 * unit, 4 * unit, 5 * unit, rows] if unit else [0, rows]
     return [slice(low, high) for low, high in zip(bounds[:-1], bounds[1:])]
 
 

time: 77.5 us -> 77.5 us (level)
  no operation moved by 1% of the time
where the time goes in v9:
time: 77.5 us; the launch traced here: 77.3 us
  blocking collectives  60.4 us (78%)
  Pallas kernels  15.3 us (20%)
    all_to_all x4, blocking collectives, exchange(): lax.all_to_all(pieces, 'freq', split_axis=0, concat_axis=0, tiled=True, a...  60.4 us
    pallas_call x1, Pallas kernels, final(): pl.pallas_call(final_kernel, in_specs=[VMEM] * 3, out_specs=ANY, out_shap...  4.97 us
    pallas_call x1, Pallas kernels, forward(): pl.pallas_call(lambda *refs: forward_kernel(*refs, halves=halves), in_spe...  4.22 us
    pallas_call x1, Pallas kernels, middle(): pl.pallas_call(lambda *refs: middle_kernel(*refs, step=step), in_specs=[V...  3.38 us
  transfers between devices with their start and end apart: 1, of which 1 were waited for; matrix products, arithmetic and copies ran while one was open for 0% of the time, Pallas kernels for 1%

profile of v9, /device:TPU:0, one launch (start us, length us, event | category | flops | bytes accessed | tf_op | source)
XLA Modules:
  0.0 77.3 jit_solution(16085890392025889118)
XLA Ops:
  0.6 4.2 %forward_dft.1 = (bf16[32,6144]{1,0:T(8,128)(2,1)S(1)}, f32[32,6144]{1,0:T(8,128)S(1)}, bf16[6144,512]{1,0:T(8,128)(2,1)S(1)}, bf16[64,512]{1,0:T(8,128)(2,1)S(1...) custom-call(bf16[6144,512]{1,0:T(8,128)(2,1)} %bitcast.36, ...), custom_call_target="tpu_custom_call" | custom-call | tf_op jit(solution)/shard_map/forward_dft/pallas_call | solution.py:146
  4.9 0.1 pad_maximum_fusion
  5.0 18.7 %all_to_all.20 = bf16[16,5,8,384]{3,2,1,0:T(8,128)(2,1)S(1)} all-to-all(bf16[16,5,8,384]{3,2,1,0:T(8,128)(2,1)S(1)} %pad_maximum_fusion), channel_id=1, replica_groups={{11,13,15,1,3,6,5,9,2,7,4,14,8,12,10,0},{27,29,31,17,19,22,21,25,18,23,..., dimensions={0} | all-to-all | bytes 983040 | tf_op jit(solution)/shard_map/all_to_all | solution.py:354
  23.7 0.2 collective-permute-start
  24.0 0.8 %owner_products.1.refs_0_ = f32[512,384]{1,0:T(8,128)S(1)} custom-call(bf16[512,384]{1,0:T(8,128)(2,1)S(1)} %bitcast.30, bf16[512,512]{1,0:T(8,128)(2,1)S(1)} %get-tuple-element.19.operator_ref, f32[1536,128]{1,0:T(8,128)S(1)} %get-tuple-element.20.recorded_ref), custom_call_target="tpu_custom_call" | custom-call | flops 402653184 | bytes 1572864 | tf_op jit(solution)/shard_map/owner_products/pallas_call | solution.py:299
  24.8 0.3 collective-permute-done.refs_2_
  25.1 0.6 smooth_sources.1
  25.7 13.9 %all_to_all.21 = bf16[16,2,16,384]{3,2,1,0:T(8,128)(2,1)S(1)} all-to-all(bf16[16,2,16,384]{3,2,1,0:T(8,128)(2,1)S(1)} %get-tuple-element.22), channel_id=1, replica_groups={{11,13,15,1,3,6,5,9,2,7,4,14,8,12,10,0},{27,29,31,17,19,22,21,25,18,23,..., dimensions={0} | all-to-all | bytes 786432 | tf_op jit(solution)/shard_map/all_to_all | solution.py:354
  39.6 0.1 copy.18
  39.7 3.4 %update_and_forward.1 = (f32[6144,512]{1,0:T(8,128)S(1)}, bf16[32,6144]{1,0:T(8,128)(2,1)S(1)}) custom-call(bf16[6144,512]{1,0:T(8,128)(2,1)S(1)} %get-tuple-element.16.refs_0_, bf16[32,6144]{1,0:T(8,128)(2,1)S(1)} %bitcast.29, f32[32,6144]{1,0:T(8,128)S(1)} %get-tuple-element.23.refs_2_, bf16[64,512]{1,0:T(8,128)(2,1)S(1)} %get-tuple-element.24.refs_3_.table_ref), custom_call_target="tpu_custom_call" | custom-call | tf_op jit(solution)/shard_map/update_and_forward/pallas_call | solution.py:194
  43.1 13.9 %all_to_all.22.arrived_ref = bf16[16,2,16,384]{3,2,1,0:T(8,128)(2,1)S(1)} all-to-all(bf16[16,2,16,384]{3,2,1,0:T(8,128)(2,1)S(1)} %bitcast.39), channel_id=1, replica_groups={{11,13,15,1,3,6,5,9,2,7,4,14,8,12,10,0},{27,29,31,17,19,22,21,25,18,23,..., dimensions={0} | all-to-all | bytes 786432 | tf_op jit(solution)/shard_map/all_to_all | solution.py:354
  57.0 1.3 %owner_step.1 = (bf16[16,2,16,384]{3,2,1,0:T(8,128)(2,1)S(1)}, f32[1536,128]{1,0:T(8,128)}) custom-call(bf16[16,2,16,384]{3,2,1,0:T(8,128)(2,1)S(1)} %all_to_all.22.arrived_ref, bf16[512,512]{1,0:T(8,128)(2,1)S(1)} %get-tuple-element.19.operator_ref, f32[1536,128]{1,0:T(8,128)S(1)} %get-tuple-element.20.recorded_ref, ...), custom_call_target="tpu_custom_call" | custom-call | tf_op jit(solution)/shard_map/owner_step/pallas_call | solution.py:328
  58.4 13.9 %all_to_all.23 = bf16[16,2,16,384]{3,2,1,0:T(8,128)(2,1)S(1)} all-to-all(bf16[16,2,16,384]{3,2,1,0:T(8,128)(2,1)S(1)} %get-tuple-element.28), channel_id=1, replica_groups={{11,13,15,1,3,6,5,9,2,7,4,14,8,12,10,0},{27,29,31,17,19,22,21,25,18,23,..., dimensions={0} | all-to-all | bytes 786432 | tf_op jit(solution)/shard_map/all_to_all | solution.py:354
  72.2 0.1 copy.20
  72.3 5.0 %last_update.1 = f32[6144,512]{1,0:T(8,128)} custom-call(f32[6144,512]{1,0:T(8,128)S(1)} %get-tuple-element.25.field_ref, bf16[32,6144]{1,0:T(8,128)(2,1)S(1)} %bitcast.31, bf16[64,512]{1,0:T(8,128)(2,1)S(1)} %get-tuple-element.24.refs_3_.table_ref), custom_call_target="tpu_custom_call" | custom-call | tf_op jit(solution)/shard_map/last_update/pallas_call | solution.py:226
  (5 shorter events, 0.2 us)
Async XLA Ops:
  23.7 1.4 %collective-permute-start = (bf16[16,8,384]{2,1,0:T(8,128)(2,1)S(1)}, bf16[16,8,384]{2,1,0:T(8,128)(2,1)S(1)}, u32[]{:S(2)}, u32[]{:S(2)}) collective-permute-start(bf16[16,8,384]{2,1,0:T(8,128)(2,1)S(1)} %slice_bitcast_fusion.refs_1_), channel_id=1, source_target_pairs={{0,1},{1,0},{2,3},{3,2},{4,5},{5,4},{6,7},{7,6},{8,9},{9,8},{10,11... | collective-permute-start | bytes 294920 | tf_op jit(solution)/shard_map/ppermute | solution.py:373

commit v10 on v8

--- a/solution.py
+++ b/solution.py
@@ -126,6 +126,8 @@
         transform(i)
     small[3].wait()
     recorded_ref[...] = loaded[...].astype(jnp.float32)
+    for i in range(max(1, len(parts) // 2), len(parts) - 1):
+        transform(i)
     small[4].wait()
     shares, amount = max(halves) + 1, radius_ref.shape[1]
     for share in range(shares):
@@ -133,7 +135,7 @@
         for rank, half in enumerate(halves):
             if half == share:
                 radius_ref[rank] = rows_sent.astype(jnp.bfloat16)
-    for i in range(max(1, len(parts) // 2), len(parts)):
+    for i in range(max(1, len(parts) - 1), len(parts)):
         transform(i)
     small[6].wait()
 

time: 77.5 us -> 77.5 us (level)
  no operation moved by 1% of the time
where the time goes in v10:
time: 77.5 us; the launch traced here: 77.2 us
  blocking collectives  60.4 us (78%)
  Pallas kernels  15.3 us (20%)
    all_to_all x4, blocking collectives, exchange(): lax.all_to_all(pieces, 'freq', split_axis=0, concat_axis=0, tiled=True, a...  60.4 us
    pallas_call x1, Pallas kernels, final(): pl.pallas_call(final_kernel, in_specs=[VMEM] * 3, out_specs=ANY, out_shap...  4.97 us
    pallas_call x1, Pallas kernels, forward(): pl.pallas_call(lambda *refs: forward_kernel(*refs, halves=halves), in_spe...  4.15 us
    pallas_call x1, Pallas kernels, middle(): pl.pallas_call(lambda *refs: middle_kernel(*refs, step=step), in_specs=[V...  3.38 us
  transfers between devices with their start and end apart: 1, of which 1 were waited for; matrix products, arithmetic and copies ran while one was open for 0% of the time, Pallas kernels for 1%

profile of v10, /device:TPU:0, one launch (start us, length us, event | category | flops | bytes accessed | tf_op | source)
XLA Modules:
  0.0 77.2 jit_solution(14078676614753596510)
XLA Ops:
  0.6 4.2 %forward_dft.1 = (bf16[32,6144]{1,0:T(8,128)(2,1)S(1)}, f32[32,6144]{1,0:T(8,128)S(1)}, bf16[6144,512]{1,0:T(8,128)(2,1)S(1)}, bf16[64,512]{1,0:T(8,128)(2,1)S(1...) custom-call(bf16[6144,512]{1,0:T(8,128)(2,1)} %bitcast.36, ...), custom_call_target="tpu_custom_call" | custom-call | tf_op jit(solution)/shard_map/forward_dft/pallas_call | solution.py:148
  4.8 0.1 pad_maximum_fusion
  4.9 18.7 %all_to_all.20 = bf16[16,5,8,384]{3,2,1,0:T(8,128)(2,1)S(1)} all-to-all(bf16[16,5,8,384]{3,2,1,0:T(8,128)(2,1)S(1)} %pad_maximum_fusion), channel_id=1, replica_groups={{11,13,15,1,3,6,5,9,2,7,4,14,8,12,10,0},{27,29,31,17,19,22,21,25,18,23,..., dimensions={0} | all-to-all | bytes 983040 | tf_op jit(solution)/shard_map/all_to_all | solution.py:356
  23.6 0.2 collective-permute-start
  23.9 0.8 %owner_products.1.refs_0_ = f32[512,384]{1,0:T(8,128)S(1)} custom-call(bf16[512,384]{1,0:T(8,128)(2,1)S(1)} %bitcast.30, bf16[512,512]{1,0:T(8,128)(2,1)S(1)} %get-tuple-element.19.operator_ref, f32[1536,128]{1,0:T(8,128)S(1)} %get-tuple-element.20.recorded_ref), custom_call_target="tpu_custom_call" | custom-call | flops 402653184 | bytes 1572864 | tf_op jit(solution)/shard_map/owner_products/pallas_call | solution.py:301
  24.7 0.3 collective-permute-done.refs_2_
  25.0 0.6 smooth_sources.1
  25.7 13.9 %all_to_all.21 = bf16[16,2,16,384]{3,2,1,0:T(8,128)(2,1)S(1)} all-to-all(bf16[16,2,16,384]{3,2,1,0:T(8,128)(2,1)S(1)} %get-tuple-element.22), channel_id=1, replica_groups={{11,13,15,1,3,6,5,9,2,7,4,14,8,12,10,0},{27,29,31,17,19,22,21,25,18,23,..., dimensions={0} | all-to-all | bytes 786432 | tf_op jit(solution)/shard_map/all_to_all | solution.py:356
  39.5 0.1 copy.18
  39.6 3.4 %update_and_forward.1 = (f32[6144,512]{1,0:T(8,128)S(1)}, bf16[32,6144]{1,0:T(8,128)(2,1)S(1)}) custom-call(bf16[6144,512]{1,0:T(8,128)(2,1)S(1)} %get-tuple-element.16.refs_0_, bf16[32,6144]{1,0:T(8,128)(2,1)S(1)} %bitcast.29, f32[32,6144]{1,0:T(8,128)S(1)} %get-tuple-element.23.refs_2_, bf16[64,512]{1,0:T(8,128)(2,1)S(1)} %get-tuple-element.24.refs_3_.table_ref), custom_call_target="tpu_custom_call" | custom-call | tf_op jit(solution)/shard_map/update_and_forward/pallas_call | solution.py:196
  43.1 13.9 %all_to_all.22.arrived_ref = bf16[16,2,16,384]{3,2,1,0:T(8,128)(2,1)S(1)} all-to-all(bf16[16,2,16,384]{3,2,1,0:T(8,128)(2,1)S(1)} %bitcast.39), channel_id=1, replica_groups={{11,13,15,1,3,6,5,9,2,7,4,14,8,12,10,0},{27,29,31,17,19,22,21,25,18,23,..., dimensions={0} | all-to-all | bytes 786432 | tf_op jit(solution)/shard_map/all_to_all | solution.py:356
  56.9 1.3 %owner_step.1 = (bf16[16,2,16,384]{3,2,1,0:T(8,128)(2,1)S(1)}, f32[1536,128]{1,0:T(8,128)}) custom-call(bf16[16,2,16,384]{3,2,1,0:T(8,128)(2,1)S(1)} %all_to_all.22.arrived_ref, bf16[512,512]{1,0:T(8,128)(2,1)S(1)} %get-tuple-element.19.operator_ref, f32[1536,128]{1,0:T(8,128)S(1)} %get-tuple-element.20.recorded_ref, ...), custom_call_target="tpu_custom_call" | custom-call | tf_op jit(solution)/shard_map/owner_step/pallas_call | solution.py:330
  58.3 13.9 %all_to_all.23 = bf16[16,2,16,384]{3,2,1,0:T(8,128)(2,1)S(1)} all-to-all(bf16[16,2,16,384]{3,2,1,0:T(8,128)(2,1)S(1)} %get-tuple-element.28), channel_id=1, replica_groups={{11,13,15,1,3,6,5,9,2,7,4,14,8,12,10,0},{27,29,31,17,19,22,21,25,18,23,..., dimensions={0} | all-to-all | bytes 786432 | tf_op jit(solution)/shard_map/all_to_all | solution.py:356
  72.2 0.1 copy.20
  72.2 5.0 %last_update.1 = f32[6144,512]{1,0:T(8,128)} custom-call(f32[6144,512]{1,0:T(8,128)S(1)} %get-tuple-element.25.field_ref, bf16[32,6144]{1,0:T(8,128)(2,1)S(1)} %bitcast.31, bf16[64,512]{1,0:T(8,128)(2,1)S(1)} %get-tuple-element.24.refs_3_.table_ref), custom_call_target="tpu_custom_call" | custom-call | tf_op jit(solution)/shard_map/last_update/pallas_call | solution.py:228
  (5 shorter events, 0.2 us)
Async XLA Ops:
  23.6 1.4 %collective-permute-start = (bf16[16,8,384]{2,1,0:T(8,128)(2,1)S(1)}, bf16[16,8,384]{2,1,0:T(8,128)(2,1)S(1)}, u32[]{:S(2)}, u32[]{:S(2)}) collective-permute-start(bf16[16,8,384]{2,1,0:T(8,128)(2,1)S(1)} %slice_bitcast_fusion.refs_1_), channel_id=1, source_target_pairs={{0,1},{1,0},{2,3},{3,2},{4,5},{5,4},{6,7},{7,6},{8,9},{9,8},{10,11... | collective-permute-start | bytes 294920 | tf_op jit(solution)/shard_map/ppermute | solution.py:375
